TPU v7x, 32 devices: a whole 2x2x4 slice. The times are simulated.
32 devices in a mesh: cells: 8 (over z, y), fsdp: 4 (over x, core).
Axes of the slice: x: 2, y: 2, z: 4, core: 2. Of those that a mesh axis runs over, the one named last changes fastest.
Arguments:
- tokens: bfloat16 [32, 1024, 512], P(('cells', 'fsdp')), may hold values from -6 to 6
- cotangent: bfloat16 [32, 1024, 512], P(('cells', 'fsdp')), may hold values from -6 to 6
- lengths: int32 [32], P(('cells', 'fsdp')), may hold values from 69 to 1024, as said below
- generate: int32 [32, 1024], P(('cells', 'fsdp')), may hold values 0 or 1
- qkv_weight: bfloat16 [512, 1536], P('fsdp'), may hold values from -0.25 to 0.25
- out_weight: bfloat16 [512, 512], P('fsdp'), may hold values from -2 to 2
- ff_in_weight: bfloat16 [512, 512], P('fsdp'), may hold values from -0.25 to 0.25
- ff_out_weight: bfloat16 [512, 512], P('fsdp'), may hold values from -0.25 to 0.25
- biases: bfloat16 [7, 512], P(None, 'fsdp'), may hold values from -1.75 to 1.75
- gains: bfloat16 [2, 512], P(None, 'fsdp'), may hold values from 0.25 to 1.75
Outputs:
- mixed: bfloat16 [32, 1024, 512], P(('cells', 'fsdp'))
- tokens_grad: float32 [32, 1024, 512], P(('cells', 'fsdp'))
- qkv_grad: float32 [512, 1536], P('fsdp')
- out_grad: float32 [512, 512], P('fsdp')
- ff_in_grad: float32 [512, 512], P('fsdp')
- ff_out_grad: float32 [512, 512], P('fsdp')
- biases_grad: float32 [7, 512], P(None, 'fsdp')
- gains_grad: float32 [2, 512], P(None, 'fsdp')
Inputs may be any that keep to these rules, and one draw needn't show every extreme that they name: `lengths`: some cell in every draw has exactly 1024 gene tokens.
All inputs are finite; a program needn't handle non-finite values. No bound on the sum of `generate` on one device may be relied on, other than what follows from the above.
Results may differ from a plain program's by a relative error of at most 0.015.
The roundings to bfloat16 on the way count: a program that leaves them out, or rounds other values in their place, can miss the bound.
Values may be sent and summed in bfloat16 or wider, within the bound.
A program may use at most 128 MiB of HBM per device.

v0:
```python
import jax
import jax.numpy as jnp
from jax import lax
from jax.sharding import PartitionSpec as P

H = 8
QB = 512


norm_eps = 1e-05


def layer_norm(value, gain, shift):
    centre = jnp.mean(value, axis=-1, keepdims=True)
    centred = value - centre
    spread = jnp.mean(centred * centred, axis=-1, keepdims=True)
    return centred * lax.rsqrt(spread + norm_eps) * gain + shift


def gelu_exact(value):
    return jax.nn.gelu(value, approximate=False)


def multiply(first, second):
    return jnp.dot(first, second, preferred_element_type=jnp.float32)


def multiply_first(first, second):
    return lax.dot_general(
        first, second, (((0,), (0,)), ((), ())), preferred_element_type=jnp.float32
    )


def multiply_second(first, second):
    return lax.dot_general(
        first, second, (((1,), (1,)), ((), ())), preferred_element_type=jnp.float32
    )


def allowed_mask(first_row, row_count, length, generate):
    row_ids = first_row + jnp.arange(row_count, dtype=jnp.int32)
    col_ids = jnp.arange(generate.shape[0], dtype=jnp.int32)
    visible = (col_ids < length) & (generate == 0)
    return (row_ids[:, None] == col_ids[None, :]) | visible[None, :]


def block_scores(query_part, key_part, allowed, score_scale):
    raw_scores = jnp.einsum(
        "qhd,khd->hqk", query_part, key_part, preferred_element_type=jnp.float32
    )
    return jnp.where(allowed[None], raw_scores * score_scale, -1000000000.0)


def attention_forward(queries, keys, values, length, generate):
    row_count, model_width = queries.shape
    head_size = model_width // H
    span = 2 * head_size
    score_scale = head_size ** (-0.5)
    blocks = row_count // QB

    def compute(query_block, first_row):
        allowed = allowed_mask(first_row, QB, length, generate)
        outputs = []
        sums_list = []
        for pair_index in range(H // 2):
            first_col = pair_index * span
            query_part = query_block[:, first_col : first_col + span].reshape(QB, 2, head_size)
            key_part = keys[:, first_col : first_col + span].reshape(row_count, 2, head_size)
            value_part = values[:, first_col : first_col + span].reshape(row_count, 2, head_size)
            scores = block_scores(query_part, key_part, allowed, score_scale)
            row_max = jnp.max(scores, axis=-1, keepdims=True)
            weights_exp = jnp.exp(scores - row_max)
            row_total = jnp.sum(weights_exp, axis=-1, keepdims=True)
            probs_low = (weights_exp / row_total).astype(jnp.bfloat16)
            mixture = jnp.einsum(
                "hqk,khd->qhd", probs_low, value_part, preferred_element_type=jnp.float32
            )
            outputs.append(mixture.reshape(QB, span))
            sums_list.append((row_max + jnp.log(row_total))[:, :, 0])
        return (jnp.concatenate(outputs, 1), jnp.concatenate(sums_list, 0))

    def one_block(inputs_block):
        query_block, first_row = inputs_block
        return compute(query_block, first_row)

    starts = jnp.arange(blocks, dtype=jnp.int32) * QB
    attended, logsum = lax.map(one_block, (queries.reshape(blocks, QB, model_width), starts))
    return (attended.reshape(row_count, model_width), logsum)


def attention_backward(queries, keys, values, logsum, grad_attended, length, generate):
    row_count, model_width = queries.shape
    head_size = model_width // H
    span = 2 * head_size
    score_scale = head_size ** (-0.5)
    blocks = row_count // QB

    def compute(query_block, grad_block, block_sums, first_row):
        allowed = allowed_mask(first_row, QB, length, generate)
        query_terms = []
        key_terms = []
        value_terms = []
        for pair_index in range(H // 2):
            first_col = pair_index * span
            query_part = query_block[:, first_col : first_col + span].reshape(QB, 2, head_size)
            key_part = keys[:, first_col : first_col + span].reshape(row_count, 2, head_size)
            value_part = values[:, first_col : first_col + span].reshape(row_count, 2, head_size)
            grad_part = grad_block[:, first_col : first_col + span].reshape(QB, 2, head_size)
            scores = block_scores(query_part, key_part, allowed, score_scale)
            probs = jnp.exp(scores - block_sums[2 * pair_index : 2 * pair_index + 2][:, :, None])
            probs_low = probs.astype(jnp.bfloat16)
            value_grad = jnp.einsum(
                "hqk,qhd->khd", probs_low, grad_part, preferred_element_type=jnp.float32
            )
            grad_probs = jnp.einsum(
                "qhd,khd->hqk", grad_part, value_part, preferred_element_type=jnp.float32
            )
            inner_sum = jnp.sum(grad_probs * probs, axis=-1, keepdims=True)
            grad_scores = (probs * (grad_probs - inner_sum)).astype(jnp.bfloat16)
            query_grad = (
                jnp.einsum(
                    "hqk,khd->qhd", grad_scores, key_part, preferred_element_type=jnp.float32
                )
                * score_scale
            )
            key_grad = (
                jnp.einsum(
                    "hqk,qhd->khd", grad_scores, query_part, preferred_element_type=jnp.float32
                )
                * score_scale
            )
            query_terms.append(query_grad.reshape(QB, span))
            key_terms.append(key_grad.reshape(row_count, span))
            value_terms.append(value_grad.reshape(row_count, span))
        return (
            jnp.concatenate(query_terms, 1),
            jnp.concatenate(key_terms, 1),
            jnp.concatenate(value_terms, 1),
        )

    def step(carry, inputs_block):
        key_total, value_total = carry
        query_block, grad_block, block_sums, first_row = inputs_block
        query_grad, key_grad, value_grad = compute(query_block, grad_block, block_sums, first_row)
        return ((key_total + key_grad, value_total + value_grad), query_grad)

    starts = jnp.arange(blocks, dtype=jnp.int32) * QB
    zeros_full = jnp.zeros((row_count, model_width), jnp.float32)
    (grad_keys, grad_values), grad_queries = lax.scan(
        step,
        (zeros_full, zeros_full),
        (
            queries.reshape(blocks, QB, model_width),
            grad_attended.reshape(blocks, QB, model_width),
            logsum,
            starts,
        ),
    )
    return (grad_queries.reshape(row_count, model_width), grad_keys, grad_values)


def body(
    tokens,
    cotangent,
    lengths,
    generate,
    qkv_weight,
    out_weight,
    ff_in_weight,
    ff_out_weight,
    biases,
    gains,
):
    shards = (qkv_weight, out_weight, ff_in_weight, ff_out_weight, biases, gains)
    gathered = (
        lax.all_gather(shards[0], "fsdp", axis=0, tiled=True),
        lax.all_gather(shards[1], "fsdp", axis=0, tiled=True),
        lax.all_gather(shards[2], "fsdp", axis=0, tiled=True),
        lax.all_gather(shards[3], "fsdp", axis=0, tiled=True),
        lax.all_gather(shards[4], "fsdp", axis=1, tiled=True),
        lax.all_gather(shards[5], "fsdp", axis=1, tiled=True),
    )
    qkv_full, out_full, ff_in_full, ff_out_full, bias_full, gain_full = gathered
    bias_values = bias_full.astype(jnp.float32)
    gain_values = gain_full.astype(jnp.float32)
    cell_tokens = tokens[0]
    cell_cot = cotangent[0].astype(jnp.float32)
    length = lengths[0]
    cell_generate = generate[0]
    row_count, model_width = cell_tokens.shape
    projected = multiply(cell_tokens, qkv_full)
    queries = (projected[:, :model_width] + bias_values[0]).astype(jnp.bfloat16)
    keys = projected[:, model_width : 2 * model_width].astype(jnp.bfloat16)
    values = (projected[:, 2 * model_width :] + bias_values[1]).astype(jnp.bfloat16)
    attended, logsum = attention_forward(queries, keys, values, length, cell_generate)
    attended_low = attended.astype(jnp.bfloat16)
    summed = cell_tokens.astype(jnp.float32) + multiply(attended_low, out_full) + bias_values[2]
    normed, norm_pull = jax.vjp(layer_norm, summed, gain_values[0], bias_values[5])
    normed_low = normed.astype(jnp.bfloat16)
    before = multiply(normed_low, ff_in_full) + bias_values[3]
    activated, gelu_pull = jax.vjp(gelu_exact, before)
    activated_low = activated.astype(jnp.bfloat16)
    second = normed + multiply(activated_low, ff_out_full) + bias_values[4]
    final, final_pull = jax.vjp(layer_norm, second, gain_values[1], bias_values[6])
    valid = (jnp.arange(row_count, dtype=jnp.int32) < length).astype(jnp.float32)[:, None]
    mixed = (final * valid).astype(jnp.bfloat16)
    qkv_back, out_back, ff_in_back, ff_out_back = (
        lax.all_gather(qkv_weight, "fsdp", axis=0, tiled=True),
        lax.all_gather(out_weight, "fsdp", axis=0, tiled=True),
        lax.all_gather(ff_in_weight, "fsdp", axis=0, tiled=True),
        lax.all_gather(ff_out_weight, "fsdp", axis=0, tiled=True),
    )
    grad_second, gain_two, shift_two = final_pull(cell_cot * valid)
    grad_feed = grad_second.astype(jnp.bfloat16)
    ff_out_term = multiply_first(activated_low, grad_feed)
    ff_bias_two = jnp.sum(grad_feed, axis=0, dtype=jnp.float32)
    (grad_before_full,) = gelu_pull(multiply_second(grad_feed, ff_out_back))
    grad_before = grad_before_full.astype(jnp.bfloat16)
    ff_in_term = multiply_first(normed_low, grad_before)
    ff_bias_one = jnp.sum(grad_before, axis=0, dtype=jnp.float32)
    grad_normed = grad_second + multiply_second(grad_before, ff_in_back)
    grad_summed, gain_one, shift_one = norm_pull(grad_normed)
    grad_branch = grad_summed.astype(jnp.bfloat16)
    out_term = multiply_first(attended_low, grad_branch)
    out_bias = jnp.sum(grad_branch, axis=0, dtype=jnp.float32)
    grad_attended = multiply_second(grad_branch, out_back).astype(jnp.bfloat16)
    grad_queries, grad_keys, grad_values = attention_backward(
        queries, keys, values, logsum, grad_attended, length, cell_generate
    )
    query_low = grad_queries.astype(jnp.bfloat16)
    value_low = grad_values.astype(jnp.bfloat16)
    grad_projected = jnp.concatenate([query_low, grad_keys.astype(jnp.bfloat16), value_low], 1)
    qkv_term = multiply_first(cell_tokens, grad_projected)
    tokens_grad = grad_summed + multiply_second(grad_projected, qkv_back)
    query_bias = jnp.sum(query_low, axis=0, dtype=jnp.float32)
    value_bias = jnp.sum(value_low, axis=0, dtype=jnp.float32)
    bias_term = jnp.stack(
        [query_bias, value_bias, out_bias, ff_bias_one, ff_bias_two, shift_one, shift_two]
    )
    gain_term = jnp.stack([gain_one, gain_two])
    cell_factor = 1.0 / (lax.axis_size("cells") * lax.axis_size("fsdp") * tokens.shape[0])
    local_terms = (
        qkv_term * cell_factor,
        out_term * cell_factor,
        ff_in_term * cell_factor,
        ff_out_term * cell_factor,
        bias_term * cell_factor,
        gain_term * cell_factor,
    )
    narrow_sums = (
        lax.psum_scatter(
            local_terms[0].astype(jnp.bfloat16), "fsdp", scatter_dimension=0, tiled=True
        ).astype(jnp.float32),
        lax.psum_scatter(
            local_terms[1].astype(jnp.bfloat16), "fsdp", scatter_dimension=0, tiled=True
        ).astype(jnp.float32),
        lax.psum_scatter(
            local_terms[2].astype(jnp.bfloat16), "fsdp", scatter_dimension=0, tiled=True
        ).astype(jnp.float32),
        lax.psum_scatter(
            local_terms[3].astype(jnp.bfloat16), "fsdp", scatter_dimension=0, tiled=True
        ).astype(jnp.float32),
        lax.psum_scatter(
            local_terms[4].astype(jnp.bfloat16), "fsdp", scatter_dimension=1, tiled=True
        ).astype(jnp.float32),
        lax.psum_scatter(
            local_terms[5].astype(jnp.bfloat16), "fsdp", scatter_dimension=1, tiled=True
        ).astype(jnp.float32),
    )
    shares = lax.psum(
        (
            narrow_sums[0],
            narrow_sums[1],
            narrow_sums[2],
            narrow_sums[3],
            narrow_sums[4],
            narrow_sums[5],
        ),
        "cells",
    )
    qkv_grad, out_grad, ff_in_grad, ff_out_grad, biases_grad, gains_grad = shares
    return (
        mixed[None],
        tokens_grad[None],
        qkv_grad,
        out_grad,
        ff_in_grad,
        ff_out_grad,
        biases_grad,
        gains_grad,
    )


def solution(mesh):
    in_specs = (
        P(("cells", "fsdp"), None, None),
        P(("cells", "fsdp"), None, None),
        P(("cells", "fsdp")),
        P(("cells", "fsdp"), None),
        P("fsdp", None),
        P("fsdp", None),
        P("fsdp", None),
        P("fsdp", None),
        P(None, "fsdp"),
        P(None, "fsdp"),
    )
    out_specs = (
        P(("cells", "fsdp"), None, None),
        P(("cells", "fsdp"), None, None),
        P("fsdp", None),
        P("fsdp", None),
        P("fsdp", None),
        P("fsdp", None),
        P(None, "fsdp"),
        P(None, "fsdp"),
    )
    return jax.shard_map(body, mesh=mesh, in_specs=in_specs, out_specs=out_specs, check_vma=False)
```

profile of v0, /device:TPU:0, one launch (start us, length us, event | category | flops | bytes accessed | tf_op | source)
XLA Modules:
  0.0 480.1 jit_solution(11519989478029643186)
XLA Ops:
  8.7 2.4 copy.55
  12.4 5.9 %all_gather.25 = bf16[2,512]{1,0:T(2,128)(2,1)S(1)} all-gather(bf16[2,128]{1,0:T(2,128)(2,1)S(1)} %copy-done.76), channel_id=1, replica_groups=mesh['cells'=8,'fsdp'=4] {'fsdp'}, dimensions={1}, use_global_device_ids=true | all-gather | bytes 2560 | tf_op jit(solution)/shard_map/all_gather | solution.py:181
  18.3 5.4 %all_gather.23 = bf16[7,512]{1,0:T(8,128)(2,1)S(1)} all-gather(bf16[7,128]{1,0:T(8,128)(2,1)S(1)} %copy-done.73), channel_id=1, replica_groups=mesh['cells'=8,'fsdp'=4] {'fsdp'}, dimensions={1}, use_global_device_ids=true | all-gather | bytes 8960 | tf_op jit(solution)/shard_map/all_gather | solution.py:180
  24.9 9.7 %all_gather.24 = bf16[512,512]{1,0:T(8,128)(2,1)} all-gather(bf16[128,512]{1,0:T(8,128)(2,1)S(1)} %copy-done.51), channel_id=1, replica_groups=mesh['cells'=8,'fsdp'=4] {'fsdp'}, dimensions={0}, use_global_device_ids=true | all-gather | bytes 655360 | tf_op jit(solution)/shard_map/all_gather | solution.py:177
  34.6 7.7 %all_gather.26 = bf16[512,512]{1,0:T(8,128)(2,1)} all-gather(bf16[128,512]{1,0:T(8,128)(2,1)S(1)} %copy-done.52), channel_id=1, replica_groups=mesh['cells'=8,'fsdp'=4] {'fsdp'}, dimensions={0}, use_global_device_ids=true | all-gather | bytes 655360 | tf_op jit(solution)/shard_map/all_gather | solution.py:178
  42.3 7.7 %all_gather.27 = bf16[512,512]{1,0:T(8,128)(2,1)} all-gather(bf16[128,512]{1,0:T(8,128)(2,1)S(1)} %copy-done.53), channel_id=1, replica_groups=mesh['cells'=8,'fsdp'=4] {'fsdp'}, dimensions={0}, use_global_device_ids=true | all-gather | bytes 655360 | tf_op jit(solution)/shard_map/all_gather | solution.py:179
  51.3 3.2 fusion.72
  54.5 2.6 copy-done.40
  57.8 3.8 fusion.52
  65.5 45.6 %while.27 = (s32[]{:T(128)}, bf16[2,512,512]{2,1,0:T(8,128)(2,1)}, f32[2,8,512]{2,1,0:T(8,128)}, s32[2]{0:T(128)}, s32[]{:T(128)}, /*index=5*/s32[1024]{0:T(1024...) while((s32[]{:T(128)}, bf16[2,512,512]{2,1,0:T(8,128)(2,1)}, ...), condition=%wide.region_9.10_spmd, body=%wide.region_0.9_spmd.sunk | while | flops 1127230976 | bytes 75671688 | solution.py:87
  73.3 3.5 fusion.274
  76.8 1.5 fusion.279
  78.3 3.5 fusion.275
  81.8 1.5 fusion.278
  84.9 1.5 fusion.276
  95.8 3.5 fusion.274
  99.3 1.5 fusion.279
  100.9 3.5 fusion.275
  104.3 1.5 fusion.278
  105.9 1.5 fusion.277
  107.4 1.5 fusion.276
  111.1 2.5 fusion.95
  115.0 5.2 %multiply_convert_fusion.5 = (bf16[1024,512]{1,0:T(8,128)(2,1)S(1)}, f32[1024,512]{1,0:T(8,128)S(1)}, f32[1024,512]{1,0:T(8,128)S(1)}) fusion(f32[512]{0:T(512)S(1)} %bitcast.512, bf16[512,512]{1,0:T(8,128)(2,1)S(1)} %copy-done.49, f32[1024,512]{0,1:T(8,128)S(1)} %get-tuple-element.389, f32[512]{0:T(512)S(1)} %bitcast.509, f32[512]{0:T(512)S(1)} %bitcast.498, ...), kind=kOutput, calls=%fused_computation.134 | convolution fusion | flops 574095360 | bytes 7878656 | tf_op jit(solution)/shard_map/dot_general | solution.py:25
  122.5 1.7 fusion.60
  124.2 2.8 convert_reduce_fusion
  126.9 2.1 convert_reduce_fusion.1
  129.0 2.4 multiply_reduce_fusion.4
  131.4 1.9 fusion.84
  134.2 2.4 convert_reduce_fusion.2
  137.6 1.7 convolution_convert_fusion
  140.4 118.9 %while.28 = (s32[]{:T(128)}, f32[1024,512]{0,1:T(8,128)}, f32[1024,512]{0,1:T(8,128)}, bf16[2,512,512]{2,1,0:T(8,128)(2,1)}, bf16[2,512,512]{1,2,0:T(8,128)(2,1)...) while((s32[]{:T(128)}, f32[1024,512]{0,1:T(8,128)}, ...), condition=%wide.region_23.24_spmd.clone, body=%wide.region_18.23_spmd.clone.sunk | while | flops 2756705792 | bytes 316796288 | solution.py:149
  145.2 1.9 constant_dynamic-slice_fusion.2
  152.1 2.1 fusion.336
  155.0 2.1 fusion.337
  157.9 2.1 fusion.335
  160.8 2.2 fusion.334
  162.9 2.8 fusion.332
  165.7 10.1 %multiply_reduce_fusion.9 = (f32[2,512]{1,0:T(2,128)S(1)}, f32[2,512]{1,0:T(2,128)S(1)}, f32[2,512]{1,0:T(2,128)}, f32[2,512]{1,0:T(2,128)}, f32[2,512,1024]{2,1,0:T(8,128)}) fusion(f32[2,512,1024]{2,1,0:T(8,128)S(1)} %fusion.323, f32[2,512]{1,0:T(2,128)S(1)} %get-tuple-element.600, pred[512,1024]{1,0:T(8,128)(4,1)S(1)} %fusion.325, ...), kind=kOutput, calls=%fused_computation.56.clone.1 | convolution fusion | flops 155185152 | bytes 34504704 | tf_op jit(solution)/shard_map/while/body/eval_jaxpr/qhd,khd->hqk/dot_general | solution.py:115
  175.8 8.4 %multiply_convert_fusion.8 = (bf16[2,512,1024]{2,1,0:T(8,128)(2,1)S(1)}, bf16[2,512,1024]{2,1,0:T(8,128)(2,1)S(1)}, bf16[2,512,1024]{2,1,0:T(8,128)(2,1)S(1)}, bf16[2,512,1024]{2,1,0:T(8,128)(2,1)S(1)}) fusion(f32[2,512,1024]{2,1,0:T(8,128)} %get-tuple-element.617, f32[2,512,1024]{2,1,0:T(8,128)S(1)} %fusion.323, ...), kind=kLoop, calls=%fused_computation.55.clone.1 | loop fusion | flops 25165824 | bytes 42500096 | tf_op jit(solution)/shard_map/while/body/eval_jaxpr/convert_element_type | solution.py:119
  189.4 2.2 convolution_multiply_fusion.21
  194.2 2.7 maximum_add_fusion.3
  204.4 1.9 constant_dynamic-slice_fusion.2
  211.3 2.1 fusion.336
  214.2 2.1 fusion.337
  217.1 2.1 fusion.335
  220.0 2.2 fusion.334
  222.2 2.8 fusion.332
  225.0 10.1 %multiply_reduce_fusion.9 = (f32[2,512]{1,0:T(2,128)S(1)}, f32[2,512]{1,0:T(2,128)S(1)}, f32[2,512]{1,0:T(2,128)}, f32[2,512]{1,0:T(2,128)}, f32[2,512,1024]{2,1,0:T(8,128)}) fusion(f32[2,512,1024]{2,1,0:T(8,128)S(1)} %fusion.323, f32[2,512]{1,0:T(2,128)S(1)} %get-tuple-element.600, pred[512,1024]{1,0:T(8,128)(4,1)S(1)} %fusion.325, ...), kind=kOutput, calls=%fused_computation.56.clone.1 | convolution fusion | flops 155185152 | bytes 34504704 | tf_op jit(solution)/shard_map/while/body/eval_jaxpr/qhd,khd->hqk/dot_general | solution.py:115
  235.1 8.4 %multiply_convert_fusion.8 = (bf16[2,512,1024]{2,1,0:T(8,128)(2,1)S(1)}, bf16[2,512,1024]{2,1,0:T(8,128)(2,1)S(1)}, bf16[2,512,1024]{2,1,0:T(8,128)(2,1)S(1)}, bf16[2,512,1024]{2,1,0:T(8,128)(2,1)S(1)}) fusion(f32[2,512,1024]{2,1,0:T(8,128)} %get-tuple-element.617, f32[2,512,1024]{2,1,0:T(8,128)S(1)} %fusion.323, ...), kind=kLoop, calls=%fused_computation.55.clone.1 | loop fusion | flops 25165824 | bytes 42500096 | tf_op jit(solution)/shard_map/while/body/eval_jaxpr/convert_element_type | solution.py:119
  248.7 2.2 convolution_multiply_fusion.21
  253.4 2.7 maximum_add_fusion.3
  260.8 1.9 copy.63
  264.0 2.8 fusion.68
  266.9 3.1 fusion.69
  270.1 3.3 fusion.67
  274.8 3.7 fusion.50
  278.5 1.6 copy.70
  282.0 5.5 %add_bitcast_fusion = f32[1,1024,512]{1,2,0:T(8,128)} fusion(f32[1024,512]{0,1:T(8,128)S(1)} %copy-done.39, bf16[512,1536]{1,0:T(8,128)(2,1)} %all-gather.2.cloned.1.call-done, bf16[1024,512]{1,0:T(8,128)(2,1)} %copy-done.42, bf16[1024,512]{1,0:T(8,128)(2,1)} %copy.62, bf16[1024,512]{1,0:T(8,128)(2,1)} %bitcast.477, f32[1024]{0:T(1024)S(1)} %copy-done.59), kind=kOutput, calls=%fused_computation.128 | convolution fusion | flops 1621098496 | bytes 8916992 | tf_op jit(solution)/shard_map/dot_general | solution.py:35
  287.6 2.9 copy.66
  292.1 15.6 %reduce-scatter.15.cloned.1.call-done = bf16[128,512]{1,0:T(8,128)(2,1)} async-done(((bf16[512,512]{1,0:T(8,128)(2,1)}), bf16[128,512]{1,0:T(8,128)(2,1)}) %reduce-scatter.15.cloned.1.call-update) | async-done | bytes 131088 | tf_op jit(solution)/shard_map/reduce_scatter | solution.py:257
  307.7 24.2 %reduce-scatter.17.cloned.1.call-done = bf16[128,512]{1,0:T(8,128)(2,1)} async-done(((bf16[512,512]{1,0:T(8,128)(2,1)}), bf16[128,512]{1,0:T(8,128)(2,1)}) %reduce-scatter.17.cloned.1.call-update) | async-done | bytes 131088 | tf_op jit(solution)/shard_map/reduce_scatter | solution.py:260
  331.9 24.6 %reduce-scatter.13.cloned.1.call-done = bf16[128,512]{1,0:T(8,128)(2,1)} async-done(((bf16[512,512]{1,0:T(8,128)(2,1)}), bf16[128,512]{1,0:T(8,128)(2,1)}) %reduce-scatter.13.cloned.1.call-update) | async-done | bytes 131088 | tf_op jit(solution)/shard_map/reduce_scatter | solution.py:254
  356.5 30.9 %reduce-scatter.19.cloned.1.call-done = bf16[128,1536]{1,0:T(8,128)(2,1)} async-done(((bf16[512,1536]{1,0:T(8,128)(2,1)}), bf16[128,1536]{1,0:T(8,128)(2,1)}) %reduce-scatter.19.cloned.1.call-update) | async-done | bytes 393232
  388.6 83.3 %all-reduce.2 = (f32[128,1536]{0,1:T(8,128)S(1)}, f32[128,512]{1,0:T(8,128)}, f32[128,512]{1,0:T(8,128)}, f32[128,512]{1,0:T(8,128)}, f32[7,128]{1,0:T(8,128)}, /*index=5*/f32[2,128]{1,0:T(2,128)}) all-reduce(bf16[128,1536]{0,1:T(8,128)(2,1)S(1)} %copy.71, ...), channel_id=1, replica_groups=mesh['cells'=8,'fsdp'=4] {'cells'}, use_global_device_ids=true, to_apply=%region_25.26 | all-reduce | flops 394368 | bytes 2366208 | tf_op jit(solution)/shard_map/psum | solution.py:270
  (376 shorter events, 90.1 us)
Async XLA Ops:
  7.2 3.9 copy-start.46
  7.2 44.1 %all-gather.2.cloned.1.call-start = ((), (), s32[]{:S(2)}) async-start(), calls=%async_computation.6 | async-start | bytes 1966080 | tf_op jit(solution)/shard_map/all_gather | solution.py:176
  7.9 282.5 %reduce-scatter.23.cloned.1.call-start = ((), (), s32[]{:S(2)}) async-start(), calls=%async_computation.12 | async-start | bytes 163840
  8.6 3.7 copy-start.76
  8.6 9.7 %copy-start.73 = (bf16[7,128]{1,0:T(8,128)(2,1)S(1)}, bf16[7,128]{1,0:T(8,128)(2,1)}, u32[]{:S(2)}) copy-start(bf16[7,128]{1,0:T(8,128)(2,1)} %param.22) | copy-start | bytes 5380
  8.7 16.3 %copy-start.51 = (bf16[128,512]{1,0:T(8,128)(2,1)S(1)}, bf16[128,512]{1,0:T(8,128)(2,1)}, u32[]{:S(2)}) copy-start(bf16[128,512]{1,0:T(8,128)(2,1)} %param.19) | copy-start | bytes 393220
  8.7 25.9 %copy-start.52 = (bf16[128,512]{1,0:T(8,128)(2,1)S(1)}, bf16[128,512]{1,0:T(8,128)(2,1)}, u32[]{:S(2)}) copy-start(bf16[128,512]{1,0:T(8,128)(2,1)} %param.20) | copy-start | bytes 393220
  11.1 31.3 %copy-start.53 = (bf16[128,512]{1,0:T(8,128)(2,1)S(1)}, bf16[128,512]{1,0:T(8,128)(2,1)}, u32[]{:S(2)}) copy-start(bf16[128,512]{1,0:T(8,128)(2,1)} %param.21) | copy-start | bytes 393220
  65.5 45.6 %copy-start.72 = (f32[1,512]{1,0:T(1,128)S(1)}, f32[1,512]{1,0:T(1,128)}, u32[]{:S(2)}) copy-start(f32[1,512]{1,0:T(1,128)} %get-tuple-element.381) | copy-start | bytes 6148
  113.6 17.8 %copy-start.37 = (f32[1024,512]{0,1:T(8,128)}, f32[1024,512]{0,1:T(8,128)S(1)}, u32[]{:S(2)}) copy-start(f32[1024,512]{0,1:T(8,128)S(1)} %get-tuple-element.389) | copy-start | bytes 6291460
  113.6 17.8 %copy-start.55 = (f32[1024]{0:T(1024)}, f32[1024]{0:T(1024)S(1)}, u32[]{:S(2)}) copy-start(f32[1024]{0:T(1024)S(1)} %broadcast_multiply_fusion.1) | copy-start | bytes 12292
  113.9 17.5 %copy-start.60 = (f32[1024]{0:T(1024)}, f32[1024]{0:T(1024)S(1)}, u32[]{:S(2)}) copy-start(f32[1024]{0:T(1024)S(1)} %fusion.76) | copy-start | bytes 12292
  115.0 5.2 %copy-start.50 = (bf16[512,512]{1,0:T(8,128)(2,1)S(1)}, bf16[512,512]{1,0:T(8,128)(2,1)}, u32[]{:S(2)}) copy-start(bf16[512,512]{1,0:T(8,128)(2,1)} %all_gather.27) | copy-start | bytes 1572868
  115.0 5.2 %copy-start.71 = (f32[1,512]{1,0:T(1,128)S(1)}, f32[1,512]{1,0:T(1,128)}, u32[]{:S(2)}) copy-start(f32[1,512]{1,0:T(1,128)} %get-tuple-element.378) | copy-start | bytes 6148
  133.3 4.3 copy-start.48
  133.3 6.1 %copy-start.58 = (f32[1024]{0:T(1024)}, f32[1024]{0:T(1024)S(1)}, u32[]{:S(2)}) copy-start(f32[1024]{0:T(1024)S(1)} %negate_multiply_fusion.1) | copy-start | bytes 12292
  134.2 157.1 %reduce-scatter.21.cloned.1.call-start = ((), (), s32[]{:S(2)}) async-start(), calls=%async_computation.11 | async-start | bytes 163840
  140.6 9.0 %copy-start.7 = (bf16[1024,512]{0,1:T(8,128)(2,1)}, bf16[1024,512]{0,1:T(8,128)(2,1)S(1)}, u32[]{:S(2)}) copy-start(bf16[1024,512]{0,1:T(8,128)(2,1)S(1)} %get-tuple-element.703) | copy-start | bytes 3145732 | tf_op jit(solution)/shard_map/while
  140.6 9.1 %copy-start.5 = (bf16[1024,512]{0,1:T(8,128)(2,1)}, bf16[1024,512]{0,1:T(8,128)(2,1)S(1)}, u32[]{:S(2)}) copy-start(bf16[1024,512]{0,1:T(8,128)(2,1)S(1)} %get-tuple-element.700) | copy-start | bytes 3145732 | tf_op jit(solution)/shard_map/while
  148.3 6.6 %copy-start.32 = (bf16[512,128]{0,1:T(8,128)(2,1)}, bf16[512,128]{0,1:T(8,128)(2,1)S(1)}, u32[]{:S(2)}) copy-start(bf16[512,128]{0,1:T(8,128)(2,1)S(1)} %get-tuple-element.615) | copy-start | bytes 393220 | tf_op jit(solution)/shard_map/while
  149.5 4.7 copy-start.23
  149.5 7.6 %copy-start.27 = (bf16[512,128]{0,1:T(8,128)(2,1)}, bf16[512,128]{0,1:T(8,128)(2,1)S(1)}, u32[]{:S(2)}) copy-start(bf16[512,128]{0,1:T(8,128)(2,1)S(1)} %get-tuple-element.609) | copy-start | bytes 393220 | tf_op jit(solution)/shard_map/while
  149.6 10.5 %copy-start.29 = (bf16[512,128]{0,1:T(8,128)(2,1)}, bf16[512,128]{0,1:T(8,128)(2,1)S(1)}, u32[]{:S(2)}) copy-start(bf16[512,128]{0,1:T(8,128)(2,1)S(1)} %get-tuple-element.597) | copy-start | bytes 393220 | tf_op jit(solution)/shard_map/while
  149.8 4.4 copy-start.20
  149.8 7.3 %copy-start.16 = (bf16[1024,128]{0,1:T(8,128)(2,1)}, bf16[1024,128]{0,1:T(8,128)(2,1)S(1)}, u32[]{:S(2)}) copy-start(bf16[1024,128]{0,1:T(8,128)(2,1)S(1)} %get-tuple-element.610) | copy-start | bytes 786436 | tf_op jit(solution)/shard_map/while
  149.8 10.2 %copy-start.14 = (bf16[1024,128]{0,1:T(8,128)(2,1)}, bf16[1024,128]{0,1:T(8,128)(2,1)S(1)}, u32[]{:S(2)}) copy-start(bf16[1024,128]{0,1:T(8,128)(2,1)S(1)} %get-tuple-element.614) | copy-start | bytes 786436 | tf_op jit(solution)/shard_map/while
  162.9 2.8 copy-start.33
  175.8 8.5 %copy-start.21 = (bf16[1024,128]{0,1:T(8,128)(2,1)S(1)}, bf16[1024,128]{0,1:T(8,128)(2,1)}, u32[]{:S(2)}) copy-start(bf16[1024,128]{0,1:T(8,128)(2,1)} %copy-done.20) | copy-start | bytes 786436 | tf_op jit(solution)/shard_map/while
  184.3 4.1 copy-start.4
  188.4 3.3 copy-start.26
  189.4 2.8 copy-start.24
  189.4 3.3 copy-start.36
  194.1 2.8 copy-start.43
  194.2 5.7 %copy-start.6 = (bf16[1024,512]{0,1:T(8,128)(2,1)S(1)}, bf16[1024,512]{0,1:T(8,128)(2,1)}, u32[]{:S(2)}) copy-start(bf16[1024,512]{0,1:T(8,128)(2,1)} %copy-done.5) | copy-start | bytes 3145732 | tf_op jit(solution)/shard_map/while
  194.2 5.7 %copy-start.8 = (bf16[1024,512]{0,1:T(8,128)(2,1)S(1)}, bf16[1024,512]{0,1:T(8,128)(2,1)}, u32[]{:S(2)}) copy-start(bf16[1024,512]{0,1:T(8,128)(2,1)} %copy-done.7) | copy-start | bytes 3145732 | tf_op jit(solution)/shard_map/while
  199.9 9.0 %copy-start.7 = (bf16[1024,512]{0,1:T(8,128)(2,1)}, bf16[1024,512]{0,1:T(8,128)(2,1)S(1)}, u32[]{:S(2)}) copy-start(bf16[1024,512]{0,1:T(8,128)(2,1)S(1)} %get-tuple-element.703) | copy-start | bytes 3145732 | tf_op jit(solution)/shard_map/while
  199.9 9.0 %copy-start.5 = (bf16[1024,512]{0,1:T(8,128)(2,1)}, bf16[1024,512]{0,1:T(8,128)(2,1)S(1)}, u32[]{:S(2)}) copy-start(bf16[1024,512]{0,1:T(8,128)(2,1)S(1)} %get-tuple-element.700) | copy-start | bytes 3145732 | tf_op jit(solution)/shard_map/while
  207.6 6.6 %copy-start.32 = (bf16[512,128]{0,1:T(8,128)(2,1)}, bf16[512,128]{0,1:T(8,128)(2,1)S(1)}, u32[]{:S(2)}) copy-start(bf16[512,128]{0,1:T(8,128)(2,1)S(1)} %get-tuple-element.615) | copy-start | bytes 393220 | tf_op jit(solution)/shard_map/while
  208.8 4.7 copy-start.23
  208.8 7.6 %copy-start.27 = (bf16[512,128]{0,1:T(8,128)(2,1)}, bf16[512,128]{0,1:T(8,128)(2,1)S(1)}, u32[]{:S(2)}) copy-start(bf16[512,128]{0,1:T(8,128)(2,1)S(1)} %get-tuple-element.609) | copy-start | bytes 393220 | tf_op jit(solution)/shard_map/while
  208.8 10.5 %copy-start.29 = (bf16[512,128]{0,1:T(8,128)(2,1)}, bf16[512,128]{0,1:T(8,128)(2,1)S(1)}, u32[]{:S(2)}) copy-start(bf16[512,128]{0,1:T(8,128)(2,1)S(1)} %get-tuple-element.597) | copy-start | bytes 393220 | tf_op jit(solution)/shard_map/while
  209.0 4.5 copy-start.20
  209.0 7.4 %copy-start.16 = (bf16[1024,128]{0,1:T(8,128)(2,1)}, bf16[1024,128]{0,1:T(8,128)(2,1)S(1)}, u32[]{:S(2)}) copy-start(bf16[1024,128]{0,1:T(8,128)(2,1)S(1)} %get-tuple-element.610) | copy-start | bytes 786436 | tf_op jit(solution)/shard_map/while
  209.0 10.2 %copy-start.14 = (bf16[1024,128]{0,1:T(8,128)(2,1)}, bf16[1024,128]{0,1:T(8,128)(2,1)S(1)}, u32[]{:S(2)}) copy-start(bf16[1024,128]{0,1:T(8,128)(2,1)S(1)} %get-tuple-element.614) | copy-start | bytes 786436 | tf_op jit(solution)/shard_map/while
  222.2 2.8 copy-start.33
  235.1 8.5 %copy-start.21 = (bf16[1024,128]{0,1:T(8,128)(2,1)S(1)}, bf16[1024,128]{0,1:T(8,128)(2,1)}, u32[]{:S(2)}) copy-start(bf16[1024,128]{0,1:T(8,128)(2,1)} %copy-done.20) | copy-start | bytes 786436 | tf_op jit(solution)/shard_map/while
  243.5 4.1 copy-start.4
  247.6 3.3 copy-start.26
  248.7 2.8 copy-start.24
  248.7 3.3 copy-start.36
  253.4 2.8 copy-start.43
  253.4 5.7 %copy-start.6 = (bf16[1024,512]{0,1:T(8,128)(2,1)S(1)}, bf16[1024,512]{0,1:T(8,128)(2,1)}, u32[]{:S(2)}) copy-start(bf16[1024,512]{0,1:T(8,128)(2,1)} %copy-done.5) | copy-start | bytes 3145732 | tf_op jit(solution)/shard_map/while
  253.4 5.7 %copy-start.8 = (bf16[1024,512]{0,1:T(8,128)(2,1)S(1)}, bf16[1024,512]{0,1:T(8,128)(2,1)}, u32[]{:S(2)}) copy-start(bf16[1024,512]{0,1:T(8,128)(2,1)} %copy-done.7) | copy-start | bytes 3145732 | tf_op jit(solution)/shard_map/while
  260.8 3.2 copy-start.38
  260.8 3.2 copy-start.56
  260.8 3.2 copy-start.61
  260.8 3.2 copy-start.64
  260.8 3.2 copy-start.69
  262.8 12.0 %copy-start.42 = (bf16[1024,512]{1,0:T(8,128)(2,1)}, bf16[1024,512]{1,0:T(8,128)(2,1)S(1)}, u32[]{:S(2)}) copy-start(bf16[1024,512]{1,0:T(8,128)(2,1)S(1)} %copy.63) | copy-start | bytes 3145732
  263.9 43.8 %reduce-scatter.15.cloned.1.call-start = ((), (), s32[]{:S(2)}) async-start(), calls=%async_computation.8 | async-start | bytes 655360 | tf_op jit(solution)/shard_map/reduce_scatter | solution.py:257
  266.8 65.0 %reduce-scatter.17.cloned.1.call-start = ((), (), s32[]{:S(2)}) async-start(), calls=%async_computation.9 | async-start | bytes 655360 | tf_op jit(solution)/shard_map/reduce_scatter | solution.py:260
  270.0 3.4 copy-start.13
  270.0 86.5 %reduce-scatter.13.cloned.1.call-start = ((), (), s32[]{:S(2)}) async-start(), calls=%async_computation.7 | async-start | bytes 655360 | tf_op jit(solution)/shard_map/reduce_scatter | solution.py:254
  273.3 114.0 %reduce-scatter.19.cloned.1.call-start = ((), (), s32[]{:S(2)}) async-start(), calls=%async_computation.10 | async-start | bytes 1966080
  (59 other events, 108.7 us)
Sparse Core Ops, SparseCore 0:
  9.6 24.2 all-gather.1
  134.3 19.5 reduce-scatter.22
  264.0 19.6 reduce-scatter.20
  286.0 21.6 reduce-scatter.14
  310.2 21.6 reduce-scatter.16
  334.8 21.6 reduce-scatter.12
  359.2 28.1 reduce-scatter.18
where the time goes:
time: 486 us; the launch traced here: 480 us
  matrix products  126 us (26%)
  blocking collectives  120 us (25%)
  waiting for transfers between devices  96 us (20%)
  local copies, waits for them, and re-layouts  63.6 us (13%)
  other arithmetic  56.6 us (12%)
  between operations  15.6 us (3%)
    psum x1, blocking collectives, body(): lax.psum((narrow_sums[0], narrow_sums[1], narrow_sums[2], narrow_sums[3],...  83.3 us
    unnamed x10, waiting for transfers between devices  31.7 us
    dot_general x8, matrix products, compute(): jnp.einsum('qhd,khd->hqk', grad_part, value_part, preferred_element_type=...  28.7 us
    reduce_scatter x1, waiting for transfers between devices, body(): lax.psum_scatter(local_terms[1].astype(jnp.bfloat16), 'fsdp', scatter_dim...  24.6 us
    reduce_scatter x1, waiting for transfers between devices, body(): lax.psum_scatter(local_terms[3].astype(jnp.bfloat16), 'fsdp', scatter_dim...  24.2 us
    unnamed x95, local copies, waits for them, and re-layouts  21.2 us
    dot_general x16, matrix products, block_scores(): jnp.einsum('qhd,khd->hqk', query_part, key_part, preferred_element_type=j...  18.1 us
    dot_general x8, matrix products, compute(): jnp.einsum('hqk,qhd->khd', probs_low, grad_part, preferred_element_type=j...  17.2 us
  transfers between devices with their start and end apart: 7, of which 4 were waited for; matrix products, arithmetic and copies ran while one was open for 31% of the time, Pallas kernels for 0%

commit v1 on v0

v1 whole, which is shorter than its diff:
```python
import functools

import jax
import jax.numpy as jnp
from jax import lax
from jax.experimental import pallas as pl
from jax.experimental.pallas import tpu as pltpu
from jax.sharding import PartitionSpec as P

F32, BF = jnp.float32, jnp.bfloat16
MESH = pl.DeviceIdType.MESH
HEADS = 8
EPS = 1e-5
CHUNK = 384
GROUP = 8


def dot(a, b):
    return jnp.dot(a, b, preferred_element_type=F32)


def dot_t(a, b):
    return lax.dot_general(a, b, (((1,), (1,)), ((), ())), preferred_element_type=F32)


def col_sum(v):
    return jnp.sum(v, axis=0, keepdims=True)


def norm(v):
    centred = v - jnp.mean(v, axis=1, keepdims=True)
    r = lax.rsqrt(jnp.mean(centred * centred, axis=1, keepdims=True) + EPS)
    return centred * r, r


def norm_back(g, xhat, r):
    g_mean = jnp.mean(g, axis=1, keepdims=True)
    x_mean = jnp.mean(g * xhat, axis=1, keepdims=True)
    return r * (g - g_mean - xhat * x_mean)


def aligned(value, step):
    return pl.multiple_of(value, step)


def layer_kernel(
    cells, fsdp, factor,
    len_ref, gen_ref, X, COT, wq_in, wo_in, w1_in, w2_in, bias_in, gain_in,
    mixed, tgrad, qkv_out, wo_out, w1_out, w2_out, bias_out, gain_out,
    W, VEC, XT, B, qp, km, VF, e, att, rL, A5, dAx, dkacc, dvacc, vecg,
    G, R1, H, S2, R2, P3, R3, R3b, R4, V0, VR1, V1, VR2, V2, VR3,
    in_sem, gs_sem, gr_sem, vs_sem, vr_sem,
    s1s, s1r, s2s, s2r, s3s, s3r, s3bs, s3br, s4s, s4r, v1s, v1r, v2s, v2r, v3s, v3r,
):
    rows_n, width = X.shape
    pairs = HEADS // 2
    act, gf, nl, gb, gbr = (A5.at[:, pl.ds(i * width, width)] for i in range(5))
    dqkv = A5.at[:, pl.ds(0, 3 * width)]
    QB = 256
    RB = 256
    blocks = rows_n // QB
    cell = lax.axis_index("cells")
    shard = lax.axis_index("fsdp")
    group = min(GROUP, cells)
    far = cells // group
    low = lax.rem(cell, group)
    high = lax.div(cell, group)

    def near_shard(s):
        return s + 1 - 2 * lax.rem(s, 2)

    def far_shard(s):
        return s + 2 - 4 * lax.rem(lax.div(s, 2), 2)

    def fsdp_dev(s):
        return (cell, s)

    def low_dev(r):
        return (high * group + lax.rem(low + r, group), shard)

    def high_dev(r):
        return (lax.rem(high + r, far) * group + low, shard)

    s_near, s_far = near_shard(shard), far_shard(shard)
    s_diag = near_shard(s_far)

    def remote(src, dst, send, recv, device):
        return pltpu.make_async_remote_copy(
            src_ref=src, dst_ref=dst, send_sem=send, recv_sem=recv, device_id=device, device_id_type=MESH
        )

    barrier = pltpu.get_barrier_semaphore()
    for s in (s_near, s_far, s_diag):
        pl.semaphore_signal(barrier, inc=1, device_id=fsdp_dev(s), device_id_type=MESH)
    for r in range(1, group):
        pl.semaphore_signal(barrier, inc=1, device_id=low_dev(r), device_id_type=MESH)
    for r in range(1, far):
        pl.semaphore_signal(barrier, inc=1, device_id=high_dev(r), device_id_type=MESH)

    own = pl.ds(aligned(shard * 128, 128), 128)
    loads = []
    for p in range(pairs):
        for t in range(3):
            loads.append((wq_in.at[:, pl.ds(t * width + p * 128, 128)], W.at[own, pl.ds(p * CHUNK + t * 128, 128)]))
    for i, ref in enumerate((wo_in, w1_in, w2_in)):
        loads.append((ref, W.at[own, pl.ds((3 + i) * width, width)]))
    loads = [pltpu.make_async_copy(a, b, in_sem.at[i]) for i, (a, b) in enumerate(loads)]
    for copy in loads:
        copy.start()
    VEC[shard] = jnp.zeros((16, 128), F32)
    VEC[shard, 0:7, :] = bias_in[...].astype(F32)
    VEC[shard, 8:10, :] = gain_in[...].astype(F32)
    pl.semaphore_wait(barrier, fsdp - 1 + group - 1 + far - 1)

    def w_copy(c, owner, hop, device):
        part = W.at[pl.ds(aligned(owner * 128, 128), 128), pl.ds(c * CHUNK, CHUNK)]
        return remote(part, part, gs_sem.at[c, hop], gr_sem.at[c, hop], device)

    def vec_copy(i, s):
        return remote(VEC.at[shard], VEC.at[shard], vs_sem.at[i], vr_sem.at[i], fsdp_dev(s))

    for i, s in enumerate((s_near, s_far, s_diag)):
        vec_copy(i, s).start()
    chunks = 8
    for c in range(chunks):
        if c < pairs:
            for t in range(3):
                loads[3 * c + t].wait()
        if c == pairs:
            for t in range(3):
                loads[3 * pairs + t].wait()
        w_copy(c, shard, 1, fsdp_dev(s_far)).start()
        w_copy(c, shard, 0, fsdp_dev(s_near)).start()

    def w_forward(c):
        w_copy(c, shard, 1, fsdp_dev(s_far)).wait_recv()
        w_copy(c, s_far, 2, fsdp_dev(s_near)).start()

    def w_ready(c):
        w_copy(c, shard, 0, fsdp_dev(s_near)).wait_recv()
        w_copy(c, s_far, 2, fsdp_dev(s_near)).wait_recv()

    length = len_ref[0]
    XT[...] = X[...].T
    col_ids = lax.broadcasted_iota(jnp.int32, (1, rows_n), 1)
    visible = jnp.where((col_ids < length) & (gen_ref[...] == 0), 0.0, -1e9).astype(F32)

    def mask_rows(i, _):
        r = aligned(i * 128, 128)
        row_ids = lax.broadcasted_iota(jnp.int32, (128, rows_n), 0) + r
        ids = lax.broadcasted_iota(jnp.int32, (128, rows_n), 1)
        B[pl.ds(r, 128), :] = jnp.where(row_ids == ids, 0.0, visible).astype(BF)
        return 0

    lax.fori_loop(0, rows_n // 128, mask_rows, 0)
    w_forward(0)
    for i, s in enumerate((s_near, s_far, s_diag)):
        vec_copy(i, s).wait_recv()
    w_ready(0)

    def bias_row(i):
        return jnp.concatenate([VEC[s, i : i + 1, :] for s in range(fsdp)], 1)

    def forward_pair(p, _):
        pr = dot(X[...], W[:, pl.ds(aligned(p * CHUNK, 128), CHUNK)])
        q = (pr[:, :128] + VEC[p, 0:1, :]).astype(BF) * jnp.asarray(0.125, BF)
        k = pr[:, 128:256].astype(BF)
        v = (pr[:, 256:] + VEC[p, 1:2, :]).astype(BF)
        first = lax.broadcasted_iota(jnp.int32, (rows_n, 128), 1) < 64
        zero, one = jnp.zeros_like(k), jnp.ones_like(k)
        qp[p] = q
        km[2 * p] = jnp.where(first, k, zero)
        km[2 * p + 1] = jnp.where(first, zero, k)
        VF[2 * p, :, 0:128] = jnp.where(first, v, zero)
        VF[2 * p, :, 128:256] = jnp.where(first, one, zero)
        VF[2 * p + 1, :, 0:128] = jnp.where(first, zero, v)
        VF[2 * p + 1, :, 128:256] = jnp.where(first, zero, one)

        def block(b, _):
            rows = pl.ds(aligned(b * QB, QB), QB)
            qb = qp[p, rows, :]
            o = None
            for h in range(2):
                s = dot_t(qb, km[2 * p + h]) + B[rows, :].astype(F32)
                weights = jnp.exp(s - jnp.max(s, axis=1, keepdims=True)).astype(BF)
                e[2 * p + h, rows, :] = weights
                part = dot(weights, VF[2 * p + h])
                o = part if o is None else o + part
            rl = 1.0 / o[:, 128:]
            att[rows, pl.ds(aligned(p * 128, 128), 128)] = (o[:, :128] * rl).astype(BF)
            rL[p, rows, :] = rl
            return 0

        for c in range(1, pairs):
            pl.when(p == c - 1)(functools.partial(w_forward, c))
        lax.fori_loop(0, blocks, block, 0)
        for c in range(1, pairs):
            pl.when(p == c - 1)(functools.partial(w_ready, c))
        return 0

    lax.fori_loop(0, pairs, forward_pair, 0)
    for c in range(pairs, chunks):
        w_forward(c)
    for c in range(pairs, chunks):
        w_ready(c)

    wo, w1, w2 = (pl.ds((3 + i) * width, width) for i in range(3))
    vecg[...] = jnp.zeros_like(vecg)

    def rows_step(i, _):
        r0 = aligned(i * RB, RB)
        rows = pl.ds(r0, RB)
        a = att[rows, :]
        gain0, gain1 = bias_row(8), bias_row(9)
        summed = X[rows, :].astype(F32) + dot(a, W[:, wo]) + bias_row(2)
        xh1, rs1 = norm(summed)
        normed = xh1 * gain0 + bias_row(5)
        n_low = normed.astype(BF)
        before = dot(n_low, W[:, w1]) + bias_row(3)
        cdf = 0.5 * (1.0 + lax.erf(before * (2.0**-0.5)))
        pdf = jnp.exp(-0.5 * before * before) * (2.0 * jnp.pi) ** -0.5
        a_low = (before * cdf).astype(BF)
        slope = cdf + before * pdf
        second = normed + dot(a_low, W[:, w2]) + bias_row(4)
        xh2, rs2 = norm(second)
        valid = (lax.broadcasted_iota(jnp.int32, (RB, 1), 0) + r0 < length).astype(F32)
        mixed[rows, :] = ((xh2 * gain1 + bias_row(6)) * valid).astype(BF)
        g = COT[rows, :].astype(F32) * valid
        g_second = norm_back(g * gain1, xh2, rs2)
        g_feed = g_second.astype(BF)
        g_before = (slope * dot_t(g_feed, W[:, w2])).astype(BF)
        g_normed = g_second + dot_t(g_before, W[:, w1])
        g_summed = norm_back(g_normed * gain0, xh1, rs1)
        g_branch = g_summed.astype(BF)
        g_att = dot_t(g_branch, W[:, wo]).astype(BF)
        act[rows, :] = a_low
        gf[rows, :] = g_feed
        nl[rows, :] = n_low
        gb[rows, :] = g_before
        gbr[rows, :] = g_branch
        tgrad[rows, :] = g_summed
        vecg[2:3, :] += col_sum(g_branch.astype(F32))
        vecg[3:4, :] += col_sum(g_before.astype(F32))
        vecg[4:5, :] += col_sum(g_feed.astype(F32))
        vecg[5:6, :] += col_sum(g_normed)
        vecg[6:7, :] += col_sum(g)
        vecg[8:9, :] += col_sum(g_normed * xh1)
        vecg[9:10, :] += col_sum(g * xh2)
        lane = lax.broadcasted_iota(jnp.int32, (RB, 128), 1)
        same = (lax.broadcasted_iota(jnp.int32, (256, 128), 0) % 128 < 64) == (
            lax.broadcasted_iota(jnp.int32, (256, 128), 1) < 64
        )
        head_ones = jnp.where(same, 1.0, 0.0).astype(BF)
        for p in range(pairs):
            cols = slice(128 * p, 128 * p + 128)
            ga = g_att[:, cols].astype(F32)
            prod = ga * a[:, cols].astype(F32)
            hi = prod.astype(BF)
            lo = (prod - hi.astype(F32)).astype(BF)
            rl = rL[p, rows, :]
            shift = -dot(jnp.concatenate([hi, lo], 1), head_ones) * rl
            s_hi = shift.astype(BF)
            s_lo = (shift - s_hi.astype(F32)).astype(BF)
            dAx[p, rows, 0:128] = (ga * rl).astype(BF)
            dAx[p, rows, 128:256] = jnp.where(
                lane % 64 == 0, s_hi, jnp.where(lane % 64 == 1, s_lo, jnp.zeros_like(s_hi))
            )
        return 0

    lax.fori_loop(0, rows_n // RB, rows_step, 0)

    def put_terms(c, term):
        term = (term * factor).astype(BF)
        for s in range(fsdp):
            G[c, s] = term[128 * s : 128 * s + 128, :]

    def s1_copy(c, i, s):
        return remote(G.at[c, s], R1.at[c, i], s1s.at[c, i], s1r.at[c, i], fsdp_dev(s_near))

    def s1_start(c):
        s1_copy(c, 0, s_near).start()
        s1_copy(c, 1, s_diag).start()

    def s2_copy(c):
        return remote(S2.at[c], R2.at[c], s2s.at[c], s2r.at[c], fsdp_dev(s_far))

    def s2_start(c):
        s1_copy(c, 0, s_near).wait_recv()
        s1_copy(c, 1, s_diag).wait_recv()
        S2[c] = (G[c, s_far].astype(F32) + R1[c, 1].astype(F32)).astype(BF)
        s2_copy(c).start()
        H[c] = G[c, shard].astype(F32) + R1[c, 0].astype(F32)

    piece = 128 // group

    def s3_copy(c, r):
        to = lax.rem(low + r, group)
        return remote(
            P3.at[c, pl.ds(aligned(to * piece, piece), piece)], R3.at[c, r - 1], s3s.at[c, r - 1], s3r.at[c, r - 1],
            low_dev(r),
        )

    def s3_start(c):
        s2_copy(c).wait_recv()
        P3[c] = (H[c] + R2[c].astype(F32)).astype(BF)
        for r in range(1, group):
            s3_copy(c, r).start()

    own_piece = pl.ds(aligned(low * piece, piece), piece)

    def s3b_copy(c, r):
        return remote(
            R4.at[c, own_piece], R3b.at[c, r - 1], s3bs.at[c, r - 1], s3br.at[c, r - 1], high_dev(r)
        )

    def s3b_start(c):
        total = P3[c, own_piece, :].astype(F32)
        for r in range(1, group):
            s3_copy(c, r).wait_recv()
            total = total + R3[c, r - 1].astype(F32)
        R4[c, own_piece, :] = total.astype(BF)
        for r in range(1, far):
            s3b_copy(c, r).start()

    def s4_copy(c, r):
        return remote(R4.at[c, own_piece], R4.at[c, own_piece], s4s.at[c, r - 1], s4r.at[c, r - 1], low_dev(r))

    def s4_start(c):
        if far > 1:
            total = R4[c, own_piece, :].astype(F32)
            for r in range(1, far):
                s3b_copy(c, r).wait_recv()
                total = total + R3b[c, r - 1].astype(F32)
            for r in range(1, far):
                s3b_copy(c, r).wait_send()
            R4[c, own_piece, :] = total.astype(BF)
        for r in range(1, group):
            s4_copy(c, r).start()

    def s3_end(c):
        s3b_start(c)
        s4_start(c)

    def s4_end(c):
        for r in range(1, group):
            s4_copy(c, r).wait_recv()

    def each(first, last, step):
        def run(c, _):
            step(c)
            return 0

        lax.fori_loop(first, last, run, 0)

    terms = [
        dot(att[...].T, gbr[...]),
        dot(nl[...].T, gb[...]),
        dot(act[...].T, gf[...]),
    ]
    for c in range(pairs):
        parts = []
        for j in range(3 * c, 3 * c + 3):
            parts.append(terms[j // 4][:, (j % 4) * 128 : (j % 4) * 128 + 128])
        put_terms(c, jnp.concatenate(parts, 1))
        s1_start(c)

    first_n = lax.broadcasted_iota(jnp.int32, (rows_n, 128), 1) < 64

    def backward_pair(p, _):
        def block(b, _):
            rows = pl.ds(aligned(b * QB, QB), QB)
            q = qp[p, rows, :]
            da = dAx[p, rows, :]
            dq, dk, dv = None, [], []
            for h in range(2):
                shifted = dot_t(da, VF[2 * p + h])
                weights = e[2 * p + h, rows, :]
                ds = (weights.astype(F32) * shifted).astype(BF)
                part = dot(ds, km[2 * p + h])
                dq = part if dq is None else dq + part
                dk.append(dot(ds.T, q))
                dv.append(dot(weights.T, da[:, :128]))
            dkk = jnp.where(first_n, dk[0], dk[1])
            dvv = jnp.where(first_n, dv[0], dv[1])

            @pl.when(b == 0)
            def _():
                dkacc[...] = dkk
                dvacc[...] = dvv

            @pl.when(b > 0)
            def _():
                dkacc[...] += dkk
                dvacc[...] += dvv

            dqkv[rows, pl.ds(aligned(p * CHUNK, 128), 128)] = (dq * 0.125).astype(BF)
            return 0

        lax.fori_loop(0, blocks, block, 0)
        c0 = aligned(p * CHUNK, 128)
        dqkv[:, pl.ds(c0 + 128, 128)] = dkacc[...].astype(BF)
        dqkv[:, pl.ds(c0 + 256, 128)] = dvacc[...].astype(BF)
        g = dqkv[:, pl.ds(c0, CHUNK)]
        c1 = aligned(p * 128, 128)
        vecg[0:1, pl.ds(c1, 128)] = col_sum(g[:, :128].astype(F32))
        vecg[1:2, pl.ds(c1, 128)] = col_sum(g[:, 256:].astype(F32))
        put_terms(pairs + p, dot(XT[...], g))
        s1_start(pairs + p)
        pl.when(p == 0)(functools.partial(each, 0, pairs, s2_start))
        pl.when(p == 1)(functools.partial(each, 0, pairs, s3_start))
        pl.when(p == 2)(functools.partial(each, 0, pairs, s3_end))
        pl.when(p >= 1)(lambda: s2_start(pairs + p - 1))
        pl.when(p >= 2)(lambda: s3_start(pairs + p - 2))
        pl.when(p >= 3)(lambda: s3_end(pairs + p - 3))
        return 0

    lax.fori_loop(0, pairs, backward_pair, 0)

    for s in range(fsdp):
        V0[s] = vecg[:, 128 * s : 128 * s + 128] * factor

    def v1_copy(i, s):
        return remote(V0.at[s], VR1.at[i], v1s.at[i], v1r.at[i], fsdp_dev(s))

    def v2_copy(r):
        return remote(V1, VR2.at[r - 1], v2s.at[r - 1], v2r.at[r - 1], low_dev(r))

    def v3_copy(r):
        return remote(V2, VR3.at[r - 1], v3s.at[r - 1], v3r.at[r - 1], high_dev(r))

    others = (s_near, s_far, s_diag)
    for i, s in enumerate(others):
        v1_copy(i, s).start()
    last = 2 * pairs - 1
    s2_start(last)
    s3_start(last - 1)
    s3_end(last - 2)

    def tokens_step(i, _):
        rows = pl.ds(aligned(i * RB, RB), RB)
        tgrad[rows, :] += dot_t(dqkv[rows, :], W[:, 0 : 3 * width])
        return 0

    lax.fori_loop(0, rows_n // RB, tokens_step, 0)
    s3_start(last)
    for i, s in enumerate(others):
        v1_copy(i, s).wait_recv()
    V1[...] = V0[shard] + VR1[0] + VR1[1] + VR1[2]
    for r in range(1, group):
        v2_copy(r).start()
    s3_end(last - 1)
    s3_end(last)
    total = V1[...]
    for r in range(1, group):
        v2_copy(r).wait_recv()
        total = total + VR2[r - 1]
    V2[...] = total
    for r in range(1, far):
        v3_copy(r).start()
    for r in range(1, far):
        v3_copy(r).wait_recv()
        total = total + VR3[r - 1]
    bias_out[...] = total[0:7, :]
    gain_out[...] = total[8:10, :]

    each(0, 2 * pairs, s4_end)
    for p in range(pairs):
        g = R4[pairs + p].astype(F32)
        for t in range(3):
            qkv_out[:, t * width + p * 128 : t * width + p * 128 + 128] = g[:, 128 * t : 128 * t + 128]
        g = R4[p].astype(F32)
        for t in range(3):
            j = 3 * p + t
            (wo_out, w1_out, w2_out)[j // 4][:, (j % 4) * 128 : (j % 4) * 128 + 128] = g[:, 128 * t : 128 * t + 128]

    for c in range(chunks):
        w_copy(c, shard, 1, fsdp_dev(s_far)).wait_send()
        w_copy(c, shard, 0, fsdp_dev(s_near)).wait_send()
        w_copy(c, s_far, 2, fsdp_dev(s_near)).wait_send()

    def drain(c):
        s1_copy(c, 0, s_near).wait_send()
        s1_copy(c, 1, s_diag).wait_send()
        s2_copy(c).wait_send()
        for r in range(1, group):
            s3_copy(c, r).wait_send()
            s4_copy(c, r).wait_send()

    each(0, 2 * pairs, drain)
    for i, s in enumerate(others):
        vec_copy(i, s).wait_send()
        v1_copy(i, s).wait_send()
    for r in range(1, group):
        v2_copy(r).wait_send()
    for r in range(1, far):
        v3_copy(r).wait_send()


def call_layer(cells, fsdp, rows_n, width, *args):
    vm = pl.BlockSpec(memory_space=pltpu.VMEM)
    sm = pl.BlockSpec(memory_space=pltpu.SMEM)
    shard_rows = width // fsdp
    group = min(GROUP, cells)
    far = cells // group
    piece = 128 // group
    chunks = 8
    factor = 1.0 / (cells * fsdp)
    dma = pltpu.SemaphoreType.DMA
    outs = (
        ((rows_n, width), BF), ((rows_n, width), F32), ((shard_rows, 3 * width), F32), ((shard_rows, width), F32),
        ((shard_rows, width), F32), ((shard_rows, width), F32), ((7, width // fsdp), F32), ((2, width // fsdp), F32),
    )
    far_n = max(far - 1, 1)
    scratch = [
        ((width, 6 * width), BF), ((fsdp, 16, 128), F32), ((width, rows_n), BF), ((rows_n, rows_n), BF),
        ((4, rows_n, 128), BF), ((8, rows_n, 128), BF), ((8, rows_n, 256), BF), ((8, rows_n, rows_n), BF),
        ((rows_n, width), BF), ((4, rows_n, 128), F32), ((rows_n, 5 * width), BF),
        ((4, rows_n, 256), BF), ((rows_n, 128), F32), ((rows_n, 128), F32), ((16, width), F32),
        ((chunks, fsdp, 128, CHUNK), BF), ((chunks, 2, 128, CHUNK), BF), ((chunks, 128, CHUNK), F32),
        ((chunks, 128, CHUNK), BF), ((chunks, 128, CHUNK), BF), ((chunks, 128, CHUNK), BF),
        ((chunks, group - 1, piece, CHUNK), BF), ((chunks, far_n, piece, CHUNK), BF), ((chunks, 128, CHUNK), BF),
        ((fsdp, 16, 128), F32), ((fsdp - 1, 16, 128), F32), ((16, 128), F32), ((group - 1, 16, 128), F32),
        ((16, 128), F32), ((far_n, 16, 128), F32),
    ]
    sems = [
        (15,), (chunks, 3), (chunks, 3), (3,), (3,),
        (chunks, 2), (chunks, 2), (chunks,), (chunks,), (chunks, group - 1), (chunks, group - 1), (chunks, far_n),
        (chunks, far_n), (chunks, group - 1), (chunks, group - 1), (3,), (3,), (group - 1,), (group - 1,), (far_n,),
        (far_n,),
    ]
    return pl.pallas_call(
        functools.partial(layer_kernel, cells, fsdp, factor),
        out_shape=[jax.ShapeDtypeStruct(s, t) for s, t in outs],
        in_specs=[sm] + [vm] * 9,
        out_specs=[vm] * 8,
        scratch_shapes=[pltpu.VMEM(s, t) for s, t in scratch] + [dma(s) for s in sems],
        compiler_params=pltpu.CompilerParams(
            vmem_limit_bytes=63 * 2**20, collective_id=0, has_side_effects=True
        ),
        name="layer",
    )(*args)


def body(cells, fsdp, tokens, cotangent, lengths, generate, *weights):
    _, rows_n, width = tokens.shape
    mixed, tokens_grad, *grads = call_layer(
        cells, fsdp, rows_n, width, lengths, generate, tokens[0], cotangent[0], *weights
    )
    return (mixed[None], tokens_grad[None], *grads)


def solution(mesh):
    split = P(("cells", "fsdp"), None, None)
    rows, cols = P("fsdp", None), P(None, "fsdp")
    return jax.shard_map(
        functools.partial(body, mesh.shape["cells"], mesh.shape["fsdp"]),
        mesh=mesh,
        in_specs=(split, split, P(("cells", "fsdp")), P(("cells", "fsdp"), None), rows, rows, rows, rows, cols, cols),
        out_specs=(split, split, rows, rows, rows, rows, cols, cols),
        check_vma=False,
    )
```

time: 486 us -> 126 us (0.26); the launches traced: 480 us -> 125 us
  matrix products: 126 us -> 0 us
  blocking collectives: 120 us -> 0 us
  Pallas kernels: 0 us -> 116 us
  waiting for transfers between devices: 96 us -> 0 us
  other arithmetic: 56.6 us -> 0 us
  local copies, waits for them, and re-layouts: 63.6 us -> 8.25 us
  between operations: 15.6 us -> 1.31 us
    dot_general x68 -> x0, matrix products: 126 us -> none  [the longest x8 28.7 us: compute(): jnp.einsum('qhd,khd->hqk', grad_part, value_part, preferred_element_type=...]
    pallas_call x0 -> x1, Pallas kernels: none -> 116 us  [call_layer(): pl.pallas_call(functools.partial(layer_kernel, cells, fsdp, factor), out_...]
    psum x1 -> x0, blocking collectives: 83.3 us -> none  [body(): lax.psum((narrow_sums[0], narrow_sums[1], narrow_sums[2], narrow_sums[3],...]
    reduce_scatter x3 -> x0, waiting for transfers between devices: 64.4 us -> none  [the longest x1 24.6 us: body(): lax.psum_scatter(local_terms[1].astype(jnp.bfloat16), 'fsdp', scatter_dim...]
    all_gather x5 -> x0, blocking collectives: 36.5 us -> none  [the longest x1 9.68 us: body(): lax.all_gather(shards[1], 'fsdp', axis=0, tiled=True)]
    unnamed x10 -> x0, waiting for transfers between devices: 31.7 us -> none
    convert_element_type x6 -> x0, other arithmetic: 21.3 us -> none  [the longest x2 16.9 us: compute(): grad_scores = (probs * (grad_probs - inner_sum)).astype(jnp.bfloat16)]
    reduce_sum x10 -> x0, other arithmetic: 18.2 us -> none  [the longest x2 6.96 us: compute(): row_total = jnp.sum(weights_exp, axis=-1, keepdims=True)]
  transfers between devices with their start and end apart: 7 -> 0, of which waited for: 4 -> 0; matrix products, arithmetic and copies ran while one was open for 31% -> 0% of each run, Pallas kernels for 0% -> 0%
where the time goes in v1:
time: 126 us; the launch traced here: 125 us
  Pallas kernels  116 us (92%)
  local copies, waits for them, and re-layouts  8.25 us (7%)
  between operations  1.31 us (1%)
    pallas_call x1, Pallas kernels, call_layer(): pl.pallas_call(functools.partial(layer_kernel, cells, fsdp, factor), out_...  116 us
    unnamed x22, local copies, waits for them, and re-layouts  8.25 us

profile of v1, /device:TPU:0, one launch (start us, length us, event | category | flops | bytes accessed | tf_op | source)
XLA Modules:
  0.0 125.3 jit_solution(6930058042645951062)
XLA Ops:
  1.3 115.8 %layer.1 = (bf16[1024,512]{1,0:T(8,128)(2,1)}, f32[1024,512]{1,0:T(8,128)}, f32[128,1536]{1,0:T(8,128)}, f32[128,512]{1,0:T(8,128)}, f32[128,512]{1,0:T(8,128)},...) custom-call(s32[1]{0:T(128)S(6)} %copy.26.len_ref, s32[1,1024]{1,0:T(1,128)} %gen_ref.1, ...), custom_call_target="tpu_custom_call" | custom-call | tf_op jit(solution)/shard_map/layer/pallas_call | solution.py:531
  117.1 0.0 copy-start
  117.1 2.4 %copy.27 = bf16[1,1024,512]{2,1,0:T(8,128)(2,1)} copy(bf16[1,1024,512]{2,1,0:T(8,128)(2,1)} %bitcast.7) | data formatting | bytes 2097152
  119.5 0.0 copy-done
  119.5 0.0 copy-start.1
  119.5 0.0 copy-start.4
  119.5 1.3 %copy.28 = f32[1,1024,512]{2,1,0:T(8,128)} copy(f32[1,1024,512]{2,1,0:T(8,128)S(1)} %bitcast.4) | data formatting | bytes 4194304
  120.8 0.4 copy-done.1
  121.2 0.0 copy-start.3
  121.2 0.0 copy-start.2
  121.2 0.0 copy-start.5
  121.2 0.0 copy-start.6
  121.2 0.9 copy.29
  122.1 0.0 copy-done.4
  122.1 0.7 copy.30
  122.8 0.0 copy-done.3
  122.8 0.7 copy.31
  123.5 0.0 copy-done.2
  123.5 0.7 copy.32
  124.2 0.0 copy-done.5
  124.2 0.6 copy.33
  124.8 0.0 copy-done.6
  124.8 0.6 copy.34
Async XLA Ops:
  117.1 2.4 %copy-start = (f32[1024,512]{1,0:T(8,128)S(1)}, f32[1024,512]{1,0:T(8,128)}, u32[]{:S(2)}) copy-start(f32[1024,512]{1,0:T(8,128)} %get-tuple-element.17) | copy-start | bytes 6291460
  119.5 1.7 %copy-start.1 = (f32[128,1536]{1,0:T(8,128)S(1)}, f32[128,1536]{1,0:T(8,128)}, u32[]{:S(2)}) copy-start(f32[128,1536]{1,0:T(8,128)} %get-tuple-element.34) | copy-start | bytes 2359300
  119.5 2.6 %copy-start.4 = (f32[128,512]{1,0:T(8,128)S(1)}, f32[128,512]{1,0:T(8,128)}, u32[]{:S(2)}) copy-start(f32[128,512]{1,0:T(8,128)} %get-tuple-element.35) | copy-start | bytes 786436
  121.2 1.6 %copy-start.3 = (f32[128,512]{1,0:T(8,128)S(1)}, f32[128,512]{1,0:T(8,128)}, u32[]{:S(2)}) copy-start(f32[128,512]{1,0:T(8,128)} %get-tuple-element.36) | copy-start | bytes 786436
  121.2 2.3 %copy-start.2 = (f32[128,512]{1,0:T(8,128)S(1)}, f32[128,512]{1,0:T(8,128)}, u32[]{:S(2)}) copy-start(f32[128,512]{1,0:T(8,128)} %get-tuple-element.37) | copy-start | bytes 786436
  121.2 3.0 %copy-start.5 = (f32[7,128]{1,0:T(8,128)S(1)}, f32[7,128]{1,0:T(8,128)}, u32[]{:S(2)}) copy-start(f32[7,128]{1,0:T(8,128)} %get-tuple-element.38) | copy-start | bytes 10756
  121.2 3.6 %copy-start.6 = (f32[2,128]{1,0:T(2,128)S(1)}, f32[2,128]{1,0:T(2,128)}, u32[]{:S(2)}) copy-start(f32[2,128]{1,0:T(2,128)} %get-tuple-element.39) | copy-start | bytes 3076

commit v2 on v1

v2 whole, which is shorter than its diff:
```python
import functools

import jax
import jax.numpy as jnp
from jax import lax
from jax.experimental import pallas as pl
from jax.experimental.pallas import tpu as pltpu
from jax.sharding import PartitionSpec as P

F32, BF = jnp.float32, jnp.bfloat16
MESH = pl.DeviceIdType.MESH
HEADS = 8
EPS = 1e-5
CHUNK = 384
GROUP = 8


def dot(a, b):
    return jnp.dot(a, b, preferred_element_type=F32)


def dot_t(a, b):
    return lax.dot_general(a, b, (((1,), (1,)), ((), ())), preferred_element_type=F32)


def col_sum(v):
    return jnp.sum(v, axis=0, keepdims=True)


def norm(v):
    centred = v - jnp.mean(v, axis=1, keepdims=True)
    r = lax.rsqrt(jnp.mean(centred * centred, axis=1, keepdims=True) + EPS)
    return centred * r, r


def norm_back(g, xhat, r):
    g_mean = jnp.mean(g, axis=1, keepdims=True)
    x_mean = jnp.mean(g * xhat, axis=1, keepdims=True)
    return r * (g - g_mean - xhat * x_mean)


def aligned(value, step):
    return pl.multiple_of(value, step)


def layer_kernel(
    cells, fsdp, factor,
    len_ref, gen_in, tok_in, cot_in, wq_in, wo_in, w1_in, w2_in, bias_in, gain_in,
    mixed_out, tgrad_out, sums_out, vec_out,
    X, COT, GEN, W, VEC, XT, BT, qp, QTz, KN, KT, VN, VT1, e, att, OT, rL, A5, dAn, dl, Z0, Z1, dQT,
    s0, s1, m0, m1, eb0, eb1, vecg,
    G, R1, R2, R3, R3b, R4, V0, VR1, V1, VR2, V2, VR3,
    in_sem, out_sem, gs_sem, gr_sem, vs_sem, vr_sem,
    s1s, s1r, s2s, s2r, s3s, s3r, s3bs, s3br, s4s, s4r, v1s, v1r, v2s, v2r, v3s, v3r,
):
    rows_n, width = X.shape
    pairs = HEADS // 2
    RB = 256
    LB = 256
    cell = lax.axis_index("cells")
    shard = lax.axis_index("fsdp")
    group = min(GROUP, cells)
    far = cells // group
    low = lax.rem(cell, group)
    high = lax.div(cell, group)
    act, gf, nl, gb, gbr = (A5.at[:, pl.ds(i * width, width)] for i in range(5))
    dATz, mixed, tgrad = QTz, COT, BT.at[:, pl.ds(0, width)]

    def near_shard(s):
        return s + 1 - 2 * lax.rem(s, 2)

    def far_shard(s):
        return s + 2 - 4 * lax.rem(lax.div(s, 2), 2)

    def fsdp_dev(s):
        return (cell, s)

    def low_dev(r):
        return (high * group + lax.rem(low + r, group), shard)

    def high_dev(r):
        return (lax.rem(high + r, far) * group + low, shard)

    s_near, s_far = near_shard(shard), far_shard(shard)
    s_diag = near_shard(s_far)
    others = (s_near, s_far, s_diag)

    def remote(src, dst, send, recv, device):
        return pltpu.make_async_remote_copy(
            src_ref=src, dst_ref=dst, send_sem=send, recv_sem=recv, device_id=device, device_id_type=MESH
        )

    barrier = pltpu.get_barrier_semaphore()
    for s in others:
        pl.semaphore_signal(barrier, inc=1, device_id=fsdp_dev(s), device_id_type=MESH)
    for r in range(1, group):
        pl.semaphore_signal(barrier, inc=1, device_id=low_dev(r), device_id_type=MESH)
    for r in range(1, far):
        pl.semaphore_signal(barrier, inc=1, device_id=high_dev(r), device_id_type=MESH)

    own = pl.ds(aligned(shard * 128, 128), 128)
    loads = []
    for p in range(pairs):
        for t in range(3):
            loads.append((wq_in.at[:, pl.ds(t * width + p * 128, 128)], W.at[own, pl.ds(p * CHUNK + t * 128, 128)]))
    for i, ref in enumerate((wo_in, w1_in, w2_in)):
        loads.append((ref, W.at[own, pl.ds((3 + i) * width, width)]))
    loads += [(tok_in, X), (gen_in, GEN), (cot_in, COT)]
    loads = [pltpu.make_async_copy(a, b, in_sem.at[i]) for i, (a, b) in enumerate(loads)]
    for copy in loads:
        copy.start()
    VEC[shard] = jnp.zeros((16, 128), F32)
    VEC[shard, 0:7, :] = bias_in[...].astype(F32)
    VEC[shard, 8:10, :] = gain_in[...].astype(F32)

    def w_copy(c, owner, hop, device):
        cols = pl.ds(c * CHUNK, CHUNK) if c < pairs else pl.ds(3 * width, 3 * width)
        part = W.at[pl.ds(aligned(owner * 128, 128), 128), cols]
        return remote(part, part, gs_sem.at[c, hop], gr_sem.at[c, hop], device)

    def vec_copy(i, s):
        return remote(VEC.at[shard], VEC.at[shard], vs_sem.at[i], vr_sem.at[i], fsdp_dev(s))

    parts = pairs + 1

    def w_send(c):
        w_copy(c, shard, 1, fsdp_dev(s_far)).start()
        w_copy(c, shard, 0, fsdp_dev(s_near)).start()

    def w_forward(c):
        w_copy(c, shard, 1, fsdp_dev(s_far)).wait_recv()
        w_copy(c, s_far, 2, fsdp_dev(s_near)).start()

    def w_ready(c):
        w_copy(c, shard, 0, fsdp_dev(s_near)).wait_recv()
        w_copy(c, s_far, 2, fsdp_dev(s_near)).wait_recv()

    for t in range(3):
        loads[t].wait()
    pl.semaphore_wait(barrier, fsdp - 1 + group - 1 + far - 1)
    w_send(0)
    for i, s in enumerate(others):
        vec_copy(i, s).start()
    for t in range(3, 6):
        loads[t].wait()
    w_send(1)

    length = len_ref[0]
    loads[3 * pairs + 3].wait()
    loads[3 * pairs + 4].wait()
    XT[...] = X[...].T
    col_ids = lax.broadcasted_iota(jnp.int32, (1, rows_n), 1)
    visible = jnp.where((col_ids < length) & (GEN[...] == 0), 0.0, -1e9).astype(F32)
    visible = jnp.broadcast_to(visible, (8, rows_n)).T[:, 0:1]

    def mask_cols(i, _):
        c = aligned(i * 128, 128)
        keys = lax.broadcasted_iota(jnp.int32, (rows_n, 128), 0)
        queries = lax.broadcasted_iota(jnp.int32, (rows_n, 128), 1) + c
        BT[:, pl.ds(c, 128)] = jnp.where(keys == queries, 0.0, visible)
        return 0

    lax.fori_loop(0, rows_n // 128, mask_cols, 0)
    QTz[...] = jnp.zeros_like(QTz)
    VT1[...] = jnp.ones_like(VT1)
    for t in range(6, 15):
        loads[t].wait()
    w_forward(0)
    w_send(2)
    w_send(3)
    for i, s in enumerate(others):
        vec_copy(i, s).wait_recv()
    w_ready(0)

    def bias_row(i):
        return jnp.concatenate([VEC[s, i : i + 1, :] for s in range(fsdp)], 1)

    def project(p, part):
        base = p * CHUNK
        if part == 0:
            pr = dot(X[...], W[:, pl.ds(aligned(base, 128), 256)])
            q = (pr[:, :128] + VEC[p, 0:1, :]).astype(BF) * jnp.asarray(0.125, BF)
            qp[p] = q
            KN[p] = pr[:, 128:256].astype(BF)
        if part == 1:
            pr = dot(X[...], W[:, pl.ds(aligned(base + 256, 128), 128)])
            VN[p] = (pr + VEC[p, 1:2, :]).astype(BF)
            qt = qp[p].T
            QTz[2 * p, 0:64, :] = qt[0:64]
            QTz[2 * p + 1, 64:128, :] = qt[64:128]
        if part == 2:
            KT[p] = KN[p].T
            vt = VN[p].T
            VT1[2 * p, 0:64, :] = vt[0:64]
            VT1[2 * p + 1, 0:64, :] = vt[64:128]

    units = HEADS * (rows_n // LB)
    per_head = rows_n // LB
    per_pair = 2 * per_head

    def unit(u):
        return u // per_head, u // per_pair, pl.ds(aligned((u % per_head) * LB, LB), LB)

    def score(u, s_ref, m_ref):
        h, p, cols = unit(jnp.minimum(u, units - 1))
        s = dot(KN[p], QTz[h, :, cols]) + BT[:, cols]
        s_ref[...] = s
        m_ref[0:1, :] = jnp.max(s, axis=0, keepdims=True)

    def weigh(u, s_ref, m_ref, e_ref):
        h, p, cols = unit(u)
        v = jnp.exp(s_ref[...] - m_ref[0:1, :]).astype(BF)
        e[h, :, cols] = v
        e_ref[...] = v

    def mix(u, e_ref):
        h, p, cols = unit(jnp.maximum(u, 0))
        o = dot(VT1[h], e_ref[...])
        r = 1.0 / o[64:65, :]
        rL[h, 0:1, cols] = r
        OT[h, :, cols] = o[0:64, :] * r

    slots = ((s0, m0, s1, m1, eb0, eb1), (s1, m1, s0, m0, eb1, eb0))
    for i in range(3):
        project(0, i)
    score(0, s0, m0)

    def forward_pair(p, is_last):
        for c in range(1, pairs):
            pl.when(p == c - 1)(functools.partial(w_forward, c))
        for n in range(per_pair):
            sa, ma, sb, mb, ea, eb = slots[n % 2]
            if n == 4:
                for c in range(1, pairs):
                    pl.when(p == c - 1)(functools.partial(w_ready, c))
                pl.when(p == 0)(functools.partial(w_send, pairs))
                if is_last:
                    w_forward(pairs)
            if not is_last and 4 <= n < 7:
                project(p + 1, n - 4)
            u = per_pair * p + n
            score(u + 1, sb, mb)
            weigh(u, sa, ma, ea)
            mix(u - 1, eb)
        return 0

    lax.fori_loop(0, pairs - 1, lambda p, _: forward_pair(p, False), 0)
    forward_pair(pairs - 1, True)
    mix(units - 1, slots[(per_pair - 1) % 2][4])
    for p in range(pairs):
        ot = jnp.concatenate([OT[2 * p], OT[2 * p + 1]], 0).astype(BF)
        att[:, 128 * p : 128 * p + 128] = ot.T
    w_ready(pairs)
    loads[3 * pairs + 5].wait()

    wo, w1, w2 = (pl.ds((3 + i) * width, width) for i in range(3))
    vecg[...] = jnp.zeros_like(vecg)

    def rows_step(i, _):
        r0 = aligned(i * RB, RB)
        rows = pl.ds(r0, RB)
        gain0, gain1 = bias_row(8), bias_row(9)
        summed = X[rows, :].astype(F32) + dot(att[rows, :], W[:, wo]) + bias_row(2)
        xh1, rs1 = norm(summed)
        normed = xh1 * gain0 + bias_row(5)
        n_low = normed.astype(BF)
        before = dot(n_low, W[:, w1]) + bias_row(3)
        cdf = 0.5 * (1.0 + lax.erf(before * (2.0**-0.5)))
        pdf = jnp.exp(-0.5 * before * before) * (2.0 * jnp.pi) ** -0.5
        a_low = (before * cdf).astype(BF)
        slope = cdf + before * pdf
        second = normed + dot(a_low, W[:, w2]) + bias_row(4)
        xh2, rs2 = norm(second)
        valid = (lax.broadcasted_iota(jnp.int32, (RB, 1), 0) + r0 < length).astype(F32)
        g = COT[rows, :].astype(F32) * valid
        mixed[rows, :] = ((xh2 * gain1 + bias_row(6)) * valid).astype(BF)
        g_second = norm_back(g * gain1, xh2, rs2)
        g_feed = g_second.astype(BF)
        g_before = (slope * dot_t(g_feed, W[:, w2])).astype(BF)
        g_normed = g_second + dot_t(g_before, W[:, w1])
        g_summed = norm_back(g_normed * gain0, xh1, rs1)
        g_branch = g_summed.astype(BF)
        g_att = dot_t(g_branch, W[:, wo]).astype(BF)
        act[rows, :] = a_low
        gf[rows, :] = g_feed
        nl[rows, :] = n_low
        gb[rows, :] = g_before
        gbr[rows, :] = g_branch
        tgrad[rows, :] = g_summed
        vecg[2:3, :] += col_sum(g_branch.astype(F32))
        vecg[3:4, :] += col_sum(g_before.astype(F32))
        vecg[4:5, :] += col_sum(g_feed.astype(F32))
        vecg[5:6, :] += col_sum(g_normed)
        vecg[6:7, :] += col_sum(g)
        vecg[8:9, :] += col_sum(g_normed * xh1)
        vecg[9:10, :] += col_sum(g * xh2)
        for p in range(pairs):
            dAn[p, rows, :] = g_att[:, 128 * p : 128 * p + 128]
        return 0

    lax.fori_loop(0, rows_n // RB, rows_step, 0)
    mixed_copy = pltpu.make_async_copy(mixed, mixed_out, out_sem.at[0])
    mixed_copy.start()

    near, stride = min(2, group), max(group // 2, 1)
    side, place = lax.rem(low, near), lax.div(low, near)
    band = 128 // near
    piece = band // stride
    own_rows = pl.ds(aligned(side * band + place * piece, piece), piece)

    def cell_dev(side_to, place_to, s):
        return (high * group + lax.rem(place_to, stride) * near + side_to, s)

    def cols_of(c):
        if isinstance(c, tuple):
            return 4 + c[0], pl.ds(aligned(4 * width + c[0] * 256, 256), 256)
        return c, pl.ds(c * width, width)

    def s1_all(c):
        i, cols = cols_of(c)
        return [
            remote(G.at[s, :, cols], R1.at[k, :, cols], s1s.at[i, k], s1r.at[i, k], fsdp_dev(s_near))
            for k, s in enumerate((s_near, s_diag))
        ]

    def s1_start(c):
        for copy in s1_all(c):
            copy.start()

    def s2_all(c):
        i, cols = cols_of(c)
        mine = pl.ds(aligned(side * band, band), band)
        other = pl.ds(aligned((near - 1 - side) * band, band), band)
        to = near - 1 - side
        plan = [(s_far, mine, side, s_far)]
        if near > 1:
            plan += [(shard, other, to, shard), (s_far, other, to, s_far)]
        return [
            remote(G.at[s, rows, cols], R2.at[k, :, cols], s2s.at[i, k], s2r.at[i, k], cell_dev(to_side, place, s))
            for k, (s, rows, to_side, _) in enumerate(plan)
        ]

    def s2_start(c):
        i, cols = cols_of(c)
        for copy in s1_all(c):
            copy.wait_recv()
        G[s_far, :, cols] = (G[s_far, :, cols].astype(F32) + R1[1, :, cols].astype(F32)).astype(BF)
        G[shard, :, cols] = (G[shard, :, cols].astype(F32) + R1[0, :, cols].astype(F32)).astype(BF)
        for copy in s2_all(c):
            copy.start()

    def s3_one(c, r):
        i, cols = cols_of(c)
        to = lax.rem(place + r, stride)
        rows = pl.ds(aligned(side * band + to * piece, piece), piece)
        return remote(
            G.at[shard, rows, cols], R3.at[r - 1, :, cols], s3s.at[i], s3r.at[i], cell_dev(side, place + r, shard)
        )

    def s3_whole(c):
        i, cols = cols_of(c)
        part = R3.at[:, :, cols]
        return remote(part, part, s3s.at[i], s3r.at[i], cell_dev(side, place + 1, shard))

    def s3_start(c):
        i, cols = cols_of(c)
        mine = pl.ds(aligned(side * band, band), band)
        total = G[shard, mine, cols].astype(F32)
        for k, copy in enumerate(s2_all(c)):
            copy.wait_recv()
            total = total + R2[k, :, cols].astype(F32)
        G[shard, mine, cols] = total.astype(BF)
        for r in range(1, stride):
            s3_one(c, r).start()

    def far_one(c, r):
        i, cols = cols_of(c)
        return remote(R4.at[own_rows, cols], R3b.at[r - 1, :, cols], s3bs.at[i, r - 1], s3br.at[i, r - 1], high_dev(r))

    def s4_one(c, r):
        i, cols = cols_of(c)
        part = R4.at[own_rows, cols]
        return remote(part, part, s4s.at[i], s4r.at[i], low_dev(r))

    def s4_whole(c):
        i, cols = cols_of(c)
        part = R4.at[pl.ds(0, 128 - piece), cols]
        return remote(part, part, s4s.at[i], s4r.at[i], low_dev(1))

    def s4_start(c):
        i, cols = cols_of(c)
        total = G[shard, own_rows, cols].astype(F32)
        s3_whole(c).wait_recv()
        for r in range(1, stride):
            total = total + R3[r - 1, :, cols].astype(F32)
        R4[own_rows, cols] = total.astype(BF)
        if far > 1:
            for r in range(1, far):
                far_one(c, r).start()
            for r in range(1, far):
                far_one(c, r).wait_recv()
                total = total + R3b[r - 1, :, cols].astype(F32)
            for r in range(1, far):
                far_one(c, r).wait_send()
            R4[own_rows, cols] = total.astype(BF)
        for r in range(1, group):
            s4_one(c, r).start()

    def drain(c):
        for copy in s1_all(c) + s2_all(c):
            copy.wait_send()
        s3_whole(c).wait_send()
        s4_whole(c).wait_send()

    def each_pair(step):
        def run(p, _):
            step((p,))
            return 0

        lax.fori_loop(0, pairs, run, 0)

    for i, (left, right) in enumerate(((att, gbr), (nl, gb), (act, gf))):
        term = (dot(left[...].T, right[...]) * factor).astype(BF)
        for s in range(fsdp):
            G[s, :, width * i : width * i + width] = term[128 * s : 128 * s + 128, :]
        s1_start(i)
    s2_start(0)
    s2_start(1)

    def prepare(p, _):
        gt = dAn[p].T.astype(F32)
        parts = []
        for hh in range(2):
            h = 2 * p + hh
            x = (gt[64 * hh : 64 * hh + 64, :] * rL[h, 0:1, :]).astype(BF)
            dl[h, 0:1, :] = col_sum(x.astype(F32) * OT[h])
            dATz[h, 64 * hh : 64 * hh + 64, :] = x
            parts.append(x)
        dAn[p] = jnp.concatenate(parts, 0).T
        return 0

    lax.fori_loop(0, pairs, prepare, 0)
    s2_start(2)

    def score_grads(p, hh, n, z_ref):
        cols = pl.ds(n * LB, LB)
        h = 2 * p + hh
        shifted = dot(VN[p], dATz[h, :, cols]) - dl[h, 0:1, cols]
        z_ref[:, cols] = (shifted * e[h, :, cols].astype(F32)).astype(BF)

    def query_grads(p, hh, n, z_ref):
        cols = pl.ds(n * LB, LB)
        half = slice(64 * hh, 64 * hh + 64)
        dQT[p, half, cols] = (dot(KT[p, half, :], z_ref[:, cols]) * 0.125).astype(BF)

    first = lax.broadcasted_iota(jnp.int32, (LB, 128), 1) < 64
    dka = s0.at[:, pl.ds(0, 128)]

    def value_grads(p, _):
        cols = pl.ds(aligned(p * CHUNK + 256, 128), 128)
        for n in range(per_head):
            rows = pl.ds(n * LB, LB)
            dv0 = dot(e[2 * p, rows, :], dAn[p])
            dv1 = dot(e[2 * p + 1, rows, :], dAn[p])
            A5[rows, cols] = jnp.where(first, dv0, dv1).astype(BF)
        return 0

    def key_grads(p, hh, n, z_ref):
        rows = pl.ds(n * LB, LB)
        dk = dot(z_ref[rows, :], qp[p])
        if hh == 0:
            dka[rows, :] = dk
        else:
            c = aligned(p * CHUNK, 128)
            A5[rows, pl.ds(c + 128, 128)] = jnp.where(first, dka[rows, :], dk).astype(BF)

    def put_term(n, cols, source):
        G[n, :, cols] = (dot(XT[128 * n : 128 * n + 128, :], source) * factor).astype(BF)

    def pair_term(p, n):
        source = A5[:, pl.ds(aligned(p * CHUNK, 128), 256)]
        put_term(n, pl.ds(aligned(4 * width + p * 256, 256), 256), source)

    def pair_end(p):
        c = aligned(p * CHUNK, 128)
        A5[:, pl.ds(c, 128)] = dQT[p].T
        vecg[0:1, pl.ds(aligned(p * 128, 128), 128)] = col_sum(A5[:, pl.ds(c, 128)].astype(F32))

    lax.fori_loop(0, pairs, value_grads, 0)
    s3_start(0)
    all_dv = jnp.concatenate([A5[:, CHUNK * p + 256 : CHUNK * p + 384] for p in range(pairs)], 1)
    put = (dot(XT[...], all_dv) * factor).astype(BF)
    for n in range(fsdp):
        G[n, :, 3 * width : 4 * width] = put[128 * n : 128 * n + 128, :]
    s1_start(3)
    vecg[1:2, :] = col_sum(all_dv.astype(F32))

    def backward_pair(p, _):
        before = jnp.maximum(p - 1, 0)
        for n in range(per_head):
            key_grads(before, 1, n, Z1)
            if n == 0:
                query_grads(before, 1, per_head - 1, Z1)
            else:
                query_grads(p, 0, n - 1, Z0)
            score_grads(p, 0, n, Z0)
        pair_end(before)
        pl.when(p == 0)(lambda: s2_start(3))
        pl.when(p == 1)(lambda: s3_start(2))
        pl.when(p == 2)(lambda: s3_start(3))
        pl.when(p >= 2)(lambda: s2_start((p - 2,)))
        pl.when(p == 3)(lambda: s3_start((0,)))
        for n in range(per_head):
            key_grads(p, 0, n, Z0)
            if n == 0:
                query_grads(p, 0, per_head - 1, Z0)
            else:
                query_grads(p, 1, n - 1, Z1)
            score_grads(p, 1, n, Z1)
            pair_term(before, n)
        pl.when(p >= 1)(lambda: s1_start((p - 1,)))
        pl.when(p == 0)(lambda: s3_start(1))
        pl.when(p == 0)(lambda: s4_start(0))
        pl.when(p == 1)(lambda: s4_start(1))
        pl.when(p == 2)(lambda: s4_start(2))
        pl.when(p == 3)(lambda: s4_start(3))
        return 0

    lax.fori_loop(0, pairs, backward_pair, 0)
    last = pairs - 1
    for n in range(per_head):
        key_grads(last, 1, n, Z1)
    query_grads(last, 1, per_head - 1, Z1)
    pair_end(last)
    s2_start((2,))
    for n in range(per_head):
        pair_term(last, n)
    s1_start((3,))

    for s in range(fsdp):
        V0[s] = vecg[:, 128 * s : 128 * s + 128] * factor

    def v1_copy(i, s):
        return remote(V0.at[s], VR1.at[i], v1s.at[i], v1r.at[i], fsdp_dev(s))

    def v2_copy(r):
        return remote(V1, VR2.at[r - 1], v2s.at[r - 1], v2r.at[r - 1], low_dev(r))

    def v3_copy(r):
        return remote(V2, VR3.at[r - 1], v3s.at[r - 1], v3r.at[r - 1], high_dev(r))

    for i, s in enumerate(others):
        v1_copy(i, s).start()
    s3_start((1,))
    s4_start((0,))
    s2_start((3,))

    def tokens_step(i, _):
        rows = pl.ds(aligned(i * RB, RB), RB)
        tgrad[rows, :] += dot_t(A5[rows, 0 : 3 * width], W[:, 0 : 3 * width])
        return 0

    lax.fori_loop(0, rows_n // RB, tokens_step, 0)
    tgrad_copy = pltpu.make_async_copy(tgrad, tgrad_out, out_sem.at[1])
    tgrad_copy.start()
    for i, s in enumerate(others):
        v1_copy(i, s).wait_recv()
    V1[...] = V0[shard] + VR1[0] + VR1[1] + VR1[2]
    for r in range(1, group):
        v2_copy(r).start()
    s3_start((2,))
    s4_start((1,))
    s3_start((3,))
    s4_start((2,))
    total = V1[...]
    for r in range(1, group):
        v2_copy(r).wait_recv()
        total = total + VR2[r - 1]
    if far > 1:
        V2[...] = total
        for r in range(1, far):
            v3_copy(r).start()
        for r in range(1, far):
            v3_copy(r).wait_recv()
            total = total + VR3[r - 1]
    VR1[0] = total
    vec_end = pltpu.make_async_copy(VR1.at[0], vec_out, out_sem.at[2])
    vec_end.start()
    s4_start((3,))
    for c in range(4):
        s4_whole(c).wait_recv()
    each_pair(lambda c: s4_whole(c).wait_recv())
    sums_copy = pltpu.make_async_copy(R4, sums_out, out_sem.at[3])
    sums_copy.start()

    for c in range(parts):
        w_copy(c, shard, 1, fsdp_dev(s_far)).wait_send()
        w_copy(c, shard, 0, fsdp_dev(s_near)).wait_send()
        w_copy(c, s_far, 2, fsdp_dev(s_near)).wait_send()

    for c in range(4):
        drain(c)
    each_pair(drain)
    for i, s in enumerate(others):
        vec_copy(i, s).wait_send()
        v1_copy(i, s).wait_send()
    for r in range(1, group):
        v2_copy(r).wait_send()
    for r in range(1, far):
        v3_copy(r).wait_send()
    for copy in (mixed_copy, tgrad_copy, vec_end, sums_copy):
        copy.wait()


def finish_kernel(
    mixed_in, tgrad_in, sums_in, vec_in, mixed_out, tgrad_out, qkv_out, wo_out, w1_out, w2_out, bias_out, gain_out,
    M, T, R, V, Q, O, A, B, bias, gain, sem,
):
    width = M.shape[1]
    pairs = HEADS // 2
    steps = 4
    rows = M.shape[0] // steps
    ins, outs = [], []

    def start(src, dst):
        copy = pltpu.make_async_copy(src, dst, sem.at[len(ins) + len(outs)])
        copy.start()
        return copy

    for i in range(steps):
        part = pl.ds(i * rows, rows)
        ins.append(start(tgrad_in.at[part], T.at[part]))
        ins.append(start(mixed_in.at[part], M.at[part]))
    ins.append(start(sums_in, R))
    ins.append(start(vec_in, V))
    for i in range(steps):
        part = pl.ds(i * rows, rows)
        ins[2 * i].wait()
        outs.append(start(T.at[part], tgrad_out.at[part]))
        ins[2 * i + 1].wait()
        outs.append(start(M.at[part], mixed_out.at[part]))
    ins[2 * steps].wait()
    for p in range(pairs):
        for t in range(2):
            c = 4 * width + 256 * p + 128 * t
            Q[:, t * width + p * 128 : t * width + p * 128 + 128] = R[:, c : c + 128].astype(F32)
    Q[:, 2 * width :] = R[:, 3 * width : 4 * width].astype(F32)
    outs.append(start(Q, qkv_out))
    for i, ref in enumerate((O, A, B)):
        ref[...] = R[:, i * width : i * width + width].astype(F32)
    for src, dst in ((O, wo_out), (A, w1_out), (B, w2_out)):
        outs.append(start(src, dst))
    ins[2 * steps + 1].wait()
    bias[...] = V[0:7, :]
    gain[...] = V[8:10, :]
    outs.append(start(bias, bias_out))
    outs.append(start(gain, gain_out))
    for copy in outs:
        copy.wait()


def call_layer(cells, fsdp, rows_n, width, lengths, generate, *args):
    vm = pl.BlockSpec(memory_space=pltpu.VMEM)
    sm = pl.BlockSpec(memory_space=pltpu.SMEM)
    hb = pl.BlockSpec(memory_space=pl.ANY)
    hbm = pl.BlockSpec(memory_space=pltpu.HBM)
    shard_rows = width // fsdp
    group = min(GROUP, cells)
    far = cells // group
    near = min(2, group)
    stride = group // near
    band, piece = 128 // near, 128 // group
    factor = 1.0 / (cells * fsdp)
    dma = pltpu.SemaphoreType.DMA
    outs = (((rows_n, width), BF), ((rows_n, width), F32), ((128, 6 * width), BF), ((16, 128), F32))
    far_n = max(far - 1, 1)
    LB = 256
    scratch = [
        ((rows_n, width), BF), ((rows_n, width), BF), ((1, rows_n), jnp.int32),
        ((width, 6 * width), BF), ((fsdp, 16, 128), F32), ((width, rows_n), BF), ((rows_n, rows_n), F32),
        ((4, rows_n, 128), BF), ((8, 128, rows_n), BF), ((4, rows_n, 128), BF), ((4, 128, rows_n), BF),
        ((4, rows_n, 128), BF), ((8, 80, rows_n), BF), ((8, rows_n, rows_n), BF),
        ((rows_n, width), BF), ((8, 64, rows_n), F32), ((8, 8, rows_n), F32), ((rows_n, 5 * width), BF),
        ((4, rows_n, 128), BF), ((8, 8, rows_n), F32), ((rows_n, rows_n), BF), ((rows_n, rows_n), BF),
        ((4, 128, rows_n), BF),
        ((rows_n, LB), F32), ((rows_n, LB), F32), ((8, LB), F32), ((8, LB), F32), ((rows_n, LB), BF), ((rows_n, LB), BF),
        ((16, width), F32),
        ((fsdp, 128, 6 * width), BF), ((2, 128, 6 * width), BF), ((2 * near - 1, band, 6 * width), BF),
        ((max(stride - 1, 1), piece, 6 * width), BF), ((far_n, piece, 6 * width), BF), ((128, 6 * width), BF),
        ((fsdp, 16, 128), F32), ((fsdp - 1, 16, 128), F32), ((16, 128), F32), ((group - 1, 16, 128), F32),
        ((16, 128), F32), ((far_n, 16, 128), F32),
    ]
    sems = [
        (18,), (4,), (5, 3), (5, 3), (3,), (3,), (8, 2), (8, 2), (8, 2 * near - 1), (8, 2 * near - 1), (8,), (8,),
        (8, far_n), (8, far_n), (8,), (8,), (3,), (3,), (group - 1,), (group - 1,), (far_n,), (far_n,),
    ]
    results = pl.pallas_call(
        functools.partial(layer_kernel, cells, fsdp, factor),
        out_shape=[jax.ShapeDtypeStruct(s, t) for s, t in outs],
        in_specs=[sm] + [hb] * 7 + [vm] * 2,
        out_specs=[hb] * 4,
        scratch_shapes=[pltpu.VMEM(s, t) for s, t in scratch] + [dma(s) for s in sems],
        compiler_params=pltpu.CompilerParams(
            vmem_limit_bytes=63 * 2**20 + 2**19, collective_id=0, has_side_effects=True
        ),
        name="layer",
    )(lengths, generate, *args)
    finals = (
        ((rows_n, width), BF), ((rows_n, width), F32), ((shard_rows, 3 * width), F32), ((shard_rows, width), F32),
        ((shard_rows, width), F32), ((shard_rows, width), F32), ((7, width // fsdp), F32), ((2, width // fsdp), F32),
    )
    buffers = list(outs) + list(finals[2:])
    return pl.pallas_call(
        finish_kernel,
        out_shape=[jax.ShapeDtypeStruct(s, t) for s, t in finals],
        in_specs=[hbm] * 4,
        out_specs=[hbm] * 8,
        scratch_shapes=[pltpu.VMEM(s, t) for s, t in buffers] + [dma((24,))],
        compiler_params=pltpu.CompilerParams(vmem_limit_bytes=63 * 2**20),
        name="finish",
    )(*results)


def body(cells, fsdp, tokens, cotangent, lengths, generate, *weights):
    _, rows_n, width = tokens.shape
    mixed, tokens_grad, *grads = call_layer(
        cells, fsdp, rows_n, width, lengths, generate, tokens[0], cotangent[0], *weights
    )
    return (mixed[None], tokens_grad[None], *grads)


def solution(mesh):
    split = P(("cells", "fsdp"), None, None)
    rows, cols = P("fsdp", None), P(None, "fsdp")
    return jax.shard_map(
        functools.partial(body, mesh.shape["cells"], mesh.shape["fsdp"]),
        mesh=mesh,
        in_specs=(split, split, P(("cells", "fsdp")), P(("cells", "fsdp"), None), rows, rows, rows, rows, cols, cols),
        out_specs=(split, split, rows, rows, rows, rows, cols, cols),
        check_vma=False,
    )
```

time: 126 us -> 92.6 us (0.73)
  Pallas kernels: 116 us -> 91 us
  local copies, waits for them, and re-layouts: 8.25 us -> 0 us
    pallas_call x1, Pallas kernels: 116 us -> 87.1 us  [call_layer(): pl.pallas_call(functools.partial(layer_kernel, cells, fsdp, factor), out_...]
    unnamed x22 -> x0, local copies, waits for them, and re-layouts: 8.25 us -> none
    pallas_call x0 -> x1, Pallas kernels: none -> 3.81 us  [call_layer(): pl.pallas_call(finish_kernel, out_shape=[jax.ShapeDtypeStruct(s, t) for s...]
where the time goes in v2:
time: 92.6 us; the launch traced here: 92.4 us
  Pallas kernels  91 us (98%)
  between operations  1.45 us (2%)
    pallas_call x1, Pallas kernels, call_layer(): pl.pallas_call(functools.partial(layer_kernel, cells, fsdp, factor), out_...  87.1 us
    pallas_call x1, Pallas kernels, call_layer(): pl.pallas_call(finish_kernel, out_shape=[jax.ShapeDtypeStruct(s, t) for s...  3.81 us

profile of v2, /device:TPU:0, one launch (start us, length us, event | category | flops | bytes accessed | tf_op | source)
XLA Modules:
  0.0 92.4 jit_solution(2135558307865126135)
XLA Ops:
  1.3 87.1 %layer.1 = (bf16[1024,512]{1,0:T(8,128)(2,1)}, f32[1024,512]{1,0:T(8,128)}, bf16[128,3072]{1,0:T(8,128)(2,1)}, f32[16,128]{1,0:T(8,128)}) custom-call(s32[1]{0:T(128)S(6)} %copy.18.len_ref, s32[1,1024]{1,0:T(1,128)} %gen_in.1, bf16[1024,512]{1,0:T(8,128)(2,1)} %bitcast.4, bf16[1024,512]{1,0:T(8,128)(2,1)} %bitcast.5, bf16[128,1536]{1,0:T(8,128)(2,1)} %wq_in.1, ...), custom_call_target="tpu_custom_call" | custom-call | tf_op jit(solution)/shard_map/layer/pallas_call | solution.py:697
  88.4 3.8 %finish.1 = (bf16[1024,512]{1,0:T(8,128)(2,1)}, f32[1024,512]{1,0:T(8,128)}, f32[128,1536]{1,0:T(8,128)}, f32[128,512]{1,0:T(8,128)}, f32[128,512]{1,0:T(8,128)}...) custom-call(bf16[1024,512]{1,0:T(8,128)(2,1)} %get-tuple-element.20.mixed_in, ...), custom_call_target="tpu_custom_call" | custom-call | tf_op jit(solution)/shard_map/finish/pallas_call | solution.py:713

commit v3 on v2

--- a/solution.py
+++ b/solution.py
@@ -47,15 +47,15 @@
     cells, fsdp, factor,
     len_ref, gen_in, tok_in, cot_in, wq_in, wo_in, w1_in, w2_in, bias_in, gain_in,
     mixed_out, tgrad_out, sums_out, vec_out,
-    X, COT, GEN, W, VEC, XT, BT, qp, QTz, KN, KT, VN, VT1, e, att, OT, rL, A5, dAn, dl, Z0, Z1, dQT,
-    s0, s1, m0, m1, eb0, eb1, vecg,
-    G, R1, R2, R3, R3b, R4, V0, VR1, V1, VR2, V2, VR3,
+    X, COT, GEN, W, VEC, XT, VC, qp, QTz, KN, KT, VN, VT1, e, att, OT, rL, A5, dAn, dl, Z0, Z1, dQT,
+    S, MX, eb0, eb1, vecg,
+    G, R1, R2, R3, R3b, R4, R5, R6, V0, VR1, V1, VR2, V2, VR3,
     in_sem, out_sem, gs_sem, gr_sem, vs_sem, vr_sem,
-    s1s, s1r, s2s, s2r, s3s, s3r, s3bs, s3br, s4s, s4r, v1s, v1r, v2s, v2r, v3s, v3r,
+    s1s, s1r, s2s, s2r, s3s, s3r, s3bs, s3br, s4s, s4r, s5s, s5r, s6s, s6r, v1s, v1r, v2s, v2r, v3s, v3r,
 ):
     rows_n, width = X.shape
     pairs = HEADS // 2
-    RB = 256
+    RB = 512
     LB = 256
     cell = lax.axis_index("cells")
     shard = lax.axis_index("fsdp")
@@ -64,7 +64,7 @@
     low = lax.rem(cell, group)
     high = lax.div(cell, group)
     act, gf, nl, gb, gbr = (A5.at[:, pl.ds(i * width, width)] for i in range(5))
-    dATz, mixed, tgrad = QTz, COT, BT.at[:, pl.ds(0, width)]
+    dATz, mixed, tgrad = QTz, COT, S.at[:, pl.ds(0, width)]
 
     def near_shard(s):
         return s + 1 - 2 * lax.rem(s, 2)
@@ -95,6 +95,8 @@
         pl.semaphore_signal(barrier, inc=1, device_id=fsdp_dev(s), device_id_type=MESH)
     for r in range(1, group):
         pl.semaphore_signal(barrier, inc=1, device_id=low_dev(r), device_id_type=MESH)
+    for r in range(1, group):
+        pl.semaphore_signal(barrier, inc=1, device_id=(low_dev(r)[0], s_far), device_id_type=MESH)
     for r in range(1, far):
         pl.semaphore_signal(barrier, inc=1, device_id=high_dev(r), device_id_type=MESH)
 
@@ -114,7 +116,8 @@
     VEC[shard, 8:10, :] = gain_in[...].astype(F32)
 
     def w_copy(c, owner, hop, device):
-        cols = pl.ds(c * CHUNK, CHUNK) if c < pairs else pl.ds(3 * width, 3 * width)
+        whole = isinstance(c, int) and c == pairs
+        cols = pl.ds(3 * width, 3 * width) if whole else pl.ds(aligned(c * CHUNK, 128), CHUNK)
         part = W.at[pl.ds(aligned(owner * 128, 128), 128), cols]
         return remote(part, part, gs_sem.at[c, hop], gr_sem.at[c, hop], device)
 
@@ -137,7 +140,7 @@
 
     for t in range(3):
         loads[t].wait()
-    pl.semaphore_wait(barrier, fsdp - 1 + group - 1 + far - 1)
+    pl.semaphore_wait(barrier, fsdp - 1 + 2 * (group - 1) + far - 1)
     w_send(0)
     for i, s in enumerate(others):
         vec_copy(i, s).start()
@@ -151,16 +154,7 @@
     XT[...] = X[...].T
     col_ids = lax.broadcasted_iota(jnp.int32, (1, rows_n), 1)
     visible = jnp.where((col_ids < length) & (GEN[...] == 0), 0.0, -1e9).astype(F32)
-    visible = jnp.broadcast_to(visible, (8, rows_n)).T[:, 0:1]
-
-    def mask_cols(i, _):
-        c = aligned(i * 128, 128)
-        keys = lax.broadcasted_iota(jnp.int32, (rows_n, 128), 0)
-        queries = lax.broadcasted_iota(jnp.int32, (rows_n, 128), 1) + c
-        BT[:, pl.ds(c, 128)] = jnp.where(keys == queries, 0.0, visible)
-        return 0
-
-    lax.fori_loop(0, rows_n // 128, mask_cols, 0)
+    VC[...] = jnp.broadcast_to(visible, (128, rows_n)).T
     QTz[...] = jnp.zeros_like(QTz)
     VT1[...] = jnp.ones_like(VT1)
     for t in range(6, 15):
@@ -201,52 +195,61 @@
     def unit(u):
         return u // per_head, u // per_pair, pl.ds(aligned((u % per_head) * LB, LB), LB)
 
-    def score(u, s_ref, m_ref):
-        h, p, cols = unit(jnp.minimum(u, units - 1))
-        s = dot(KN[p], QTz[h, :, cols]) + BT[:, cols]
-        s_ref[...] = s
-        m_ref[0:1, :] = jnp.max(s, axis=0, keepdims=True)
-
-    def weigh(u, s_ref, m_ref, e_ref):
-        h, p, cols = unit(u)
-        v = jnp.exp(s_ref[...] - m_ref[0:1, :]).astype(BF)
-        e[h, :, cols] = v
-        e_ref[...] = v
-
-    def mix(u, e_ref):
+    def score(u, n):
+        h, p, _ = unit(jnp.minimum(u, units - 1))
+        b = n % per_head
+        raw = dot(KN[p], QTz[h, :, LB * b : LB * b + LB])
+        for r in range(per_head):
+            rows = slice(LB * r, LB * r + LB)
+            w = VC[rows, :]
+            part = raw[rows] + jnp.concatenate([w, w], 1)
+            if r == b:
+                keys = lax.broadcasted_iota(jnp.int32, (LB, LB), 0)
+                part = jnp.where(keys == lax.broadcasted_iota(jnp.int32, (LB, LB), 1), raw[rows], part)
+            S[rows, LB * (n % 4) : LB * (n % 4) + LB] = part
+
+    def peak(n):
+        MX[n % 4, 0:1, :] = jnp.max(S[:, LB * (n % 4) : LB * (n % 4) + LB], axis=0, keepdims=True)
+
+    def weigh(u, n):
+        h, p, _ = unit(u)
+        b = n % per_head
+        v = jnp.exp(S[:, LB * (n % 4) : LB * (n % 4) + LB] - MX[n % 4, 0:1, :]).astype(BF)
+        e[h, :, LB * b : LB * b + LB] = v
+        slots[n % 2][...] = v
+
+    def mix(u, n):
         h, p, cols = unit(jnp.maximum(u, 0))
-        o = dot(VT1[h], e_ref[...])
+        o = dot(VT1[h], slots[n % 2][...])
         r = 1.0 / o[64:65, :]
         rL[h, 0:1, cols] = r
         OT[h, :, cols] = o[0:64, :] * r
 
-    slots = ((s0, m0, s1, m1, eb0, eb1), (s1, m1, s0, m0, eb1, eb0))
+    slots = (eb0, eb1)
     for i in range(3):
         project(0, i)
-    score(0, s0, m0)
+    w_send(pairs)
+    score(0, 0)
+    score(1, 1)
+    peak(0)
 
     def forward_pair(p, is_last):
-        for c in range(1, pairs):
-            pl.when(p == c - 1)(functools.partial(w_forward, c))
+        w_forward(pairs if is_last else p + 1)
         for n in range(per_pair):
-            sa, ma, sb, mb, ea, eb = slots[n % 2]
-            if n == 4:
-                for c in range(1, pairs):
-                    pl.when(p == c - 1)(functools.partial(w_ready, c))
-                pl.when(p == 0)(functools.partial(w_send, pairs))
-                if is_last:
-                    w_forward(pairs)
-            if not is_last and 4 <= n < 7:
-                project(p + 1, n - 4)
+            if n == 3 and not is_last:
+                w_ready(p + 1)
+            if not is_last and 3 <= n < 6:
+                project(p + 1, n - 3)
             u = per_pair * p + n
-            score(u + 1, sb, mb)
-            weigh(u, sa, ma, ea)
-            mix(u - 1, eb)
+            score(u + 2, n + 2)
+            weigh(u, n)
+            peak(n + 1)
+            mix(u - 1, n - 1)
         return 0
 
     lax.fori_loop(0, pairs - 1, lambda p, _: forward_pair(p, False), 0)
     forward_pair(pairs - 1, True)
-    mix(units - 1, slots[(per_pair - 1) % 2][4])
+    mix(units - 1, per_pair - 1)
     for p in range(pairs):
         ot = jnp.concatenate([OT[2 * p], OT[2 * p + 1]], 0).astype(BF)
         att[:, 128 * p : 128 * p + 128] = ot.T
@@ -341,11 +344,7 @@
         ]
 
     def s2_start(c):
-        i, cols = cols_of(c)
-        for copy in s1_all(c):
-            copy.wait_recv()
-        G[s_far, :, cols] = (G[s_far, :, cols].astype(F32) + R1[1, :, cols].astype(F32)).astype(BF)
-        G[shard, :, cols] = (G[shard, :, cols].astype(F32) + R1[0, :, cols].astype(F32)).astype(BF)
+        pair_sum(c)
         for copy in s2_all(c):
             copy.start()
 
@@ -354,15 +353,16 @@
         to = lax.rem(place + r, stride)
         rows = pl.ds(aligned(side * band + to * piece, piece), piece)
         return remote(
-            G.at[shard, rows, cols], R3.at[r - 1, :, cols], s3s.at[i], s3r.at[i], cell_dev(side, place + r, shard)
+            G.at[shard, rows, cols], R3.at[pl.ds((r - 1) * piece, piece), cols], s3s.at[i], s3r.at[i],
+            cell_dev(side, place + r, shard),
         )
 
     def s3_whole(c):
         i, cols = cols_of(c)
-        part = R3.at[:, :, cols]
+        part = R3.at[:, cols]
         return remote(part, part, s3s.at[i], s3r.at[i], cell_dev(side, place + 1, shard))
 
-    def s3_start(c):
+    def band_sum(c):
         i, cols = cols_of(c)
         mine = pl.ds(aligned(side * band, band), band)
         total = G[shard, mine, cols].astype(F32)
@@ -370,12 +370,82 @@
             copy.wait_recv()
             total = total + R2[k, :, cols].astype(F32)
         G[shard, mine, cols] = total.astype(BF)
+
+    def s3_start(c):
+        band_sum(c)
         for r in range(1, stride):
             s3_one(c, r).start()
 
-    def far_one(c, r):
-        i, cols = cols_of(c)
-        return remote(R4.at[own_rows, cols], R3b.at[r - 1, :, cols], s3bs.at[i, r - 1], s3br.at[i, r - 1], high_dev(r))
+    odd = lax.rem(place, 2)
+    beside = place + 1 - 2 * odd
+    half = 2 * piece
+    half_rows = pl.ds(aligned(side * band + odd * half, half), half)
+
+    def h3_copy(c):
+        i, cols = cols_of(c)
+        rows = pl.ds(aligned(side * band + (1 - odd) * half, half), half)
+        return remote(
+            G.at[shard, rows, cols], R3.at[pl.ds(0, half), cols], s3s.at[i], s3r.at[i], cell_dev(side, beside, shard)
+        )
+
+    def h3_start(c):
+        band_sum(c)
+        h3_copy(c).start()
+
+    def h4_copy(c):
+        i, cols = cols_of(c)
+        return remote(
+            G.at[shard, half_rows, cols], R5.at[:, cols], s5s.at[i], s5r.at[i], cell_dev(side, place + 2, shard)
+        )
+
+    def h4_start(c):
+        i, cols = cols_of(c)
+        h3_copy(c).wait_recv()
+        G[shard, half_rows, cols] = (
+            G[shard, half_rows, cols].astype(F32) + R3[0:half, cols].astype(F32)
+        ).astype(BF)
+        h4_copy(c).start()
+
+    def h5_all(c):
+        i, cols = cols_of(c)
+        part = R4.at[half_rows, cols]
+        to = near - 1 - side
+        return [
+            remote(part, part, s4s.at[i], s4r.at[i], cell_dev(a, b, shard))
+            for a, b in ((side, beside), (to, place), (to, beside))
+        ]
+
+    def h5_whole(c):
+        i, cols = cols_of(c)
+        part = R4.at[pl.ds(0, 3 * half), cols]
+        return remote(part, part, s4s.at[i], s4r.at[i], cell_dev(side, beside, shard))
+
+    def h5_start(c):
+        i, cols = cols_of(c)
+        h4_copy(c).wait_recv()
+        total = G[shard, half_rows, cols].astype(F32) + R5[:, cols].astype(F32)
+        R4[half_rows, cols] = total.astype(BF)
+        if far > 1:
+            for r in range(1, far):
+                far_one(c, r, half_rows, half).start()
+            for r in range(1, far):
+                far_one(c, r, half_rows, half).wait_recv()
+                total = total + far_slot(c, r, half)[...].astype(F32)
+            for r in range(1, far):
+                far_one(c, r, half_rows, half).wait_send()
+            R4[half_rows, cols] = total.astype(BF)
+        for copy in h5_all(c):
+            copy.start()
+
+    def far_slot(c, r, count):
+        i, cols = cols_of(c)
+        return R3b.at[r - 1, pl.ds(0, count), pl.ds((i % 2) * width, 256 if isinstance(c, tuple) else width)]
+
+    def far_one(c, r, rows, count):
+        i, cols = cols_of(c)
+        return remote(
+            R4.at[rows, cols], far_slot(c, r, count), s3bs.at[i, r - 1], s3br.at[i, r - 1], high_dev(r)
+        )
 
     def s4_one(c, r):
         i, cols = cols_of(c)
@@ -392,32 +462,75 @@
         total = G[shard, own_rows, cols].astype(F32)
         s3_whole(c).wait_recv()
         for r in range(1, stride):
-            total = total + R3[r - 1, :, cols].astype(F32)
+            total = total + R3[(r - 1) * piece : r * piece, cols].astype(F32)
+        share(c, total)
+
+    def share(c, total):
+        i, cols = cols_of(c)
         R4[own_rows, cols] = total.astype(BF)
         if far > 1:
             for r in range(1, far):
-                far_one(c, r).start()
+                far_one(c, r, own_rows, piece).start()
             for r in range(1, far):
-                far_one(c, r).wait_recv()
-                total = total + R3b[r - 1, :, cols].astype(F32)
+                far_one(c, r, own_rows, piece).wait_recv()
+                total = total + far_slot(c, r, piece)[...].astype(F32)
             for r in range(1, far):
-                far_one(c, r).wait_send()
+                far_one(c, r, own_rows, piece).wait_send()
             R4[own_rows, cols] = total.astype(BF)
         for r in range(1, group):
             s4_one(c, r).start()
 
-    def drain(c):
-        for copy in s1_all(c) + s2_all(c):
-            copy.wait_send()
-        s3_whole(c).wait_send()
-        s4_whole(c).wait_send()
-
-    def each_pair(step):
-        def run(p, _):
-            step((p,))
-            return 0
-
-        lax.fori_loop(0, pairs, run, 0)
+    def d_one(c, k, s):
+        i, cols = cols_of(c)
+        to = lax.rem(low + k, group)
+        rows = pl.ds(aligned(lax.rem(to, near) * band + lax.div(to, near) * piece, piece), piece)
+        slot = k - 1 if s is shard else group - 1 + k
+        return remote(G.at[s, rows, cols], R6.at[slot], s6s.at[0], s6r.at[0], (high * group + to, s))
+
+    def d_all(c):
+        return [d_one(c, k, s_far) for k in range(group)] + [d_one(c, k, shard) for k in range(1, group)]
+
+    def d_whole(c):
+        return remote(R6, R6, s6s.at[0], s6r.at[0], low_dev(1))
+
+    def pair_sum(c):
+        i, cols = cols_of(c)
+        for copy in s1_all(c):
+            copy.wait_recv()
+        G[s_far, :, cols] = (G[s_far, :, cols].astype(F32) + R1[1, :, cols].astype(F32)).astype(BF)
+        G[shard, :, cols] = (G[shard, :, cols].astype(F32) + R1[0, :, cols].astype(F32)).astype(BF)
+
+    def d_start(c):
+        pair_sum(c)
+        for copy in d_all(c):
+            copy.start()
+
+    def d4_start(c):
+        i, cols = cols_of(c)
+        total = G[shard, own_rows, cols].astype(F32)
+        d_whole(c).wait_recv()
+        for k in range(2 * group - 1):
+            total = total + R6[k].astype(F32)
+        share(c, total)
+
+    halved = [0, 1, 2, 3, (0,), (1,)]
+    direct = [(2,), (3,)]
+
+    def drain():
+        for c in halved + direct:
+            for copy in s1_all(c):
+                copy.wait_send()
+        for c in halved + direct[:1]:
+            for copy in s2_all(c):
+                copy.wait_send()
+        for c in halved:
+            h3_copy(c).wait_send()
+            h4_copy(c).wait_send()
+            h5_whole(c).wait_send()
+        s3_whole(direct[0]).wait_send()
+        d_whole(direct[1]).wait_send()
+        for c in direct:
+            s4_whole(c).wait_send()
 
     for i, (left, right) in enumerate(((att, gbr), (nl, gb), (act, gf))):
         term = (dot(left[...].T, right[...]) * factor).astype(BF)
@@ -425,7 +538,6 @@
             G[s, :, width * i : width * i + width] = term[128 * s : 128 * s + 128, :]
         s1_start(i)
     s2_start(0)
-    s2_start(1)
 
     def prepare(p, _):
         gt = dAn[p].T.astype(F32)
@@ -440,6 +552,7 @@
         return 0
 
     lax.fori_loop(0, pairs, prepare, 0)
+    s2_start(1)
     s2_start(2)
 
     def score_grads(p, hh, n, z_ref):
@@ -451,10 +564,10 @@
     def query_grads(p, hh, n, z_ref):
         cols = pl.ds(n * LB, LB)
         half = slice(64 * hh, 64 * hh + 64)
-        dQT[p, half, cols] = (dot(KT[p, half, :], z_ref[:, cols]) * 0.125).astype(BF)
+        dQT[lax.rem(p, 2), half, cols] = (dot(KT[p, half, :], z_ref[:, cols]) * 0.125).astype(BF)
 
     first = lax.broadcasted_iota(jnp.int32, (LB, 128), 1) < 64
-    dka = s0.at[:, pl.ds(0, 128)]
+    dka = S.at[:, pl.ds(width, 128)]
 
     def value_grads(p, _):
         cols = pl.ds(aligned(p * CHUNK + 256, 128), 128)
@@ -474,24 +587,23 @@
             c = aligned(p * CHUNK, 128)
             A5[rows, pl.ds(c + 128, 128)] = jnp.where(first, dka[rows, :], dk).astype(BF)
 
-    def put_term(n, cols, source):
-        G[n, :, cols] = (dot(XT[128 * n : 128 * n + 128, :], source) * factor).astype(BF)
-
-    def pair_term(p, n):
-        source = A5[:, pl.ds(aligned(p * CHUNK, 128), 256)]
-        put_term(n, pl.ds(aligned(4 * width + p * 256, 256), 256), source)
+    def put_terms(first_col, source):
+        term = (dot(XT[...], source) * factor).astype(BF)
+        for n in range(fsdp):
+            G[n, :, pl.ds(first_col, source.shape[1])] = term[128 * n : 128 * n + 128, :]
+
+    def pair_term(p):
+        put_terms(aligned(4 * width + p * 256, 256), A5[:, pl.ds(aligned(p * CHUNK, 128), 256)])
 
     def pair_end(p):
         c = aligned(p * CHUNK, 128)
-        A5[:, pl.ds(c, 128)] = dQT[p].T
+        A5[:, pl.ds(c, 128)] = dQT[lax.rem(p, 2)].T
         vecg[0:1, pl.ds(aligned(p * 128, 128), 128)] = col_sum(A5[:, pl.ds(c, 128)].astype(F32))
 
     lax.fori_loop(0, pairs, value_grads, 0)
-    s3_start(0)
+    h3_start(0)
     all_dv = jnp.concatenate([A5[:, CHUNK * p + 256 : CHUNK * p + 384] for p in range(pairs)], 1)
-    put = (dot(XT[...], all_dv) * factor).astype(BF)
-    for n in range(fsdp):
-        G[n, :, 3 * width : 4 * width] = put[128 * n : 128 * n + 128, :]
+    put_terms(3 * width, all_dv)
     s1_start(3)
     vecg[1:2, :] = col_sum(all_dv.astype(F32))
 
@@ -506,10 +618,13 @@
             score_grads(p, 0, n, Z0)
         pair_end(before)
         pl.when(p == 0)(lambda: s2_start(3))
-        pl.when(p == 1)(lambda: s3_start(2))
-        pl.when(p == 2)(lambda: s3_start(3))
+        pl.when(p == 1)(lambda: h3_start(2))
         pl.when(p >= 2)(lambda: s2_start((p - 2,)))
-        pl.when(p == 3)(lambda: s3_start((0,)))
+        pl.when(p == 2)(lambda: h3_start(3))
+        pl.when(p == 2)(lambda: h4_start(2))
+        pl.when(p == 3)(lambda: h3_start((0,)))
+        pl.when(p == 3)(lambda: h4_start(3))
+        pl.when(p == 3)(lambda: h5_start(2))
         for n in range(per_head):
             key_grads(p, 0, n, Z0)
             if n == 0:
@@ -517,24 +632,25 @@
             else:
                 query_grads(p, 1, n - 1, Z1)
             score_grads(p, 1, n, Z1)
-            pair_term(before, n)
-        pl.when(p >= 1)(lambda: s1_start((p - 1,)))
-        pl.when(p == 0)(lambda: s3_start(1))
-        pl.when(p == 0)(lambda: s4_start(0))
-        pl.when(p == 1)(lambda: s4_start(1))
-        pl.when(p == 2)(lambda: s4_start(2))
-        pl.when(p == 3)(lambda: s4_start(3))
+            if n == 0:
+                pair_term(before)
+            if n == 2:
+                pl.when(p >= 1)(lambda: s1_start((p - 1,)))
+        pl.when(p == 0)(lambda: h3_start(1))
+        pl.when(p == 0)(lambda: h4_start(0))
+        pl.when(p == 1)(lambda: h4_start(1))
+        pl.when(p == 1)(lambda: h5_start(0))
+        pl.when(p == 2)(lambda: h5_start(1))
         return 0
 
     lax.fori_loop(0, pairs, backward_pair, 0)
     last = pairs - 1
+    s2_start((2,))
     for n in range(per_head):
         key_grads(last, 1, n, Z1)
     query_grads(last, 1, per_head - 1, Z1)
     pair_end(last)
-    s2_start((2,))
-    for n in range(per_head):
-        pair_term(last, n)
+    pair_term(last)
     s1_start((3,))
 
     for s in range(fsdp):
@@ -551,16 +667,22 @@
 
     for i, s in enumerate(others):
         v1_copy(i, s).start()
-    s3_start((1,))
-    s4_start((0,))
-    s2_start((3,))
+    h5_start(3)
+    h3_start((1,))
+    h4_start((0,))
 
     def tokens_step(i, _):
-        rows = pl.ds(aligned(i * RB, RB), RB)
+        rows = pl.ds(aligned(i * 256, 256), 256)
         tgrad[rows, :] += dot_t(A5[rows, 0 : 3 * width], W[:, 0 : 3 * width])
         return 0
 
-    lax.fori_loop(0, rows_n // RB, tokens_step, 0)
+    steps = rows_n // 256
+    tokens_step(0, 0)
+    d_start((3,))
+    lax.fori_loop(1, steps // 2 + 1, tokens_step, 0)
+    h4_start((1,))
+    h5_start((0,))
+    lax.fori_loop(steps // 2 + 1, steps, tokens_step, 0)
     tgrad_copy = pltpu.make_async_copy(tgrad, tgrad_out, out_sem.at[1])
     tgrad_copy.start()
     for i, s in enumerate(others):
@@ -569,8 +691,8 @@
     for r in range(1, group):
         v2_copy(r).start()
     s3_start((2,))
-    s4_start((1,))
-    s3_start((3,))
+    h5_start((1,))
+    d4_start((3,))
     s4_start((2,))
     total = V1[...]
     for r in range(1, group):
@@ -586,21 +708,23 @@
     VR1[0] = total
     vec_end = pltpu.make_async_copy(VR1.at[0], vec_out, out_sem.at[2])
     vec_end.start()
-    s4_start((3,))
-    for c in range(4):
+    for c in halved:
+        h5_whole(c).wait_recv()
+    early = 5 * width
+    early_copy = pltpu.make_async_copy(R4.at[:, pl.ds(0, early)], sums_out.at[:, pl.ds(0, early)], out_sem.at[3])
+    early_copy.start()
+    for c in direct:
         s4_whole(c).wait_recv()
-    each_pair(lambda c: s4_whole(c).wait_recv())
-    sums_copy = pltpu.make_async_copy(R4, sums_out, out_sem.at[3])
-    sums_copy.start()
+    late_cols = pl.ds(early, width)
+    late_copy = pltpu.make_async_copy(R4.at[:, late_cols], sums_out.at[:, late_cols], out_sem.at[4])
+    late_copy.start()
 
     for c in range(parts):
         w_copy(c, shard, 1, fsdp_dev(s_far)).wait_send()
         w_copy(c, shard, 0, fsdp_dev(s_near)).wait_send()
         w_copy(c, s_far, 2, fsdp_dev(s_near)).wait_send()
 
-    for c in range(4):
-        drain(c)
-    each_pair(drain)
+    drain()
     for i, s in enumerate(others):
         vec_copy(i, s).wait_send()
         v1_copy(i, s).wait_send()
@@ -608,7 +732,7 @@
         v2_copy(r).wait_send()
     for r in range(1, far):
         v3_copy(r).wait_send()
-    for copy in (mixed_copy, tgrad_copy, vec_end, sums_copy):
+    for copy in (mixed_copy, tgrad_copy, vec_end, early_copy, late_copy):
         copy.wait()
 
 
@@ -677,22 +801,23 @@
     LB = 256
     scratch = [
         ((rows_n, width), BF), ((rows_n, width), BF), ((1, rows_n), jnp.int32),
-        ((width, 6 * width), BF), ((fsdp, 16, 128), F32), ((width, rows_n), BF), ((rows_n, rows_n), F32),
+        ((width, 6 * width), BF), ((fsdp, 16, 128), F32), ((width, rows_n), BF), ((rows_n, 128), F32),
         ((4, rows_n, 128), BF), ((8, 128, rows_n), BF), ((4, rows_n, 128), BF), ((4, 128, rows_n), BF),
         ((4, rows_n, 128), BF), ((8, 80, rows_n), BF), ((8, rows_n, rows_n), BF),
         ((rows_n, width), BF), ((8, 64, rows_n), F32), ((8, 8, rows_n), F32), ((rows_n, 5 * width), BF),
         ((4, rows_n, 128), BF), ((8, 8, rows_n), F32), ((rows_n, rows_n), BF), ((rows_n, rows_n), BF),
-        ((4, 128, rows_n), BF),
-        ((rows_n, LB), F32), ((rows_n, LB), F32), ((8, LB), F32), ((8, LB), F32), ((rows_n, LB), BF), ((rows_n, LB), BF),
+        ((2, 128, rows_n), BF),
+        ((rows_n, 4 * LB), F32), ((4, 8, LB), F32), ((rows_n, LB), BF), ((rows_n, LB), BF),
         ((16, width), F32),
         ((fsdp, 128, 6 * width), BF), ((2, 128, 6 * width), BF), ((2 * near - 1, band, 6 * width), BF),
-        ((max(stride - 1, 1), piece, 6 * width), BF), ((far_n, piece, 6 * width), BF), ((128, 6 * width), BF),
+        (((stride - 1) * piece, 6 * width), BF), ((far_n, 2 * piece, 2 * width), BF), ((128, 6 * width), BF),
+        ((2 * piece, 6 * width), BF), ((2 * group - 1, piece, 256), BF),
         ((fsdp, 16, 128), F32), ((fsdp - 1, 16, 128), F32), ((16, 128), F32), ((group - 1, 16, 128), F32),
         ((16, 128), F32), ((far_n, 16, 128), F32),
     ]
     sems = [
-        (18,), (4,), (5, 3), (5, 3), (3,), (3,), (8, 2), (8, 2), (8, 2 * near - 1), (8, 2 * near - 1), (8,), (8,),
-        (8, far_n), (8, far_n), (8,), (8,), (3,), (3,), (group - 1,), (group - 1,), (far_n,), (far_n,),
+        (18,), (5,), (5, 3), (5, 3), (3,), (3,), (8, 2), (8, 2), (8, 2 * near - 1), (8, 2 * near - 1), (8,), (8,),
+        (8, far_n), (8, far_n), (8,), (8,), (8,), (8,), (1,), (1,), (3,), (3,), (group - 1,), (group - 1,), (far_n,), (far_n,),
     ]
     results = pl.pallas_call(
         functools.partial(layer_kernel, cells, fsdp, factor),

time: 92.6 us -> 88.9 us (0.960)
  Pallas kernels: 91 us -> 87.3 us
    pallas_call x1, Pallas kernels: 87.1 us -> 83.5 us  [call_layer(): pl.pallas_call(functools.partial(layer_kernel, cells, fsdp, factor), out_...]
where the time goes in v3:
time: 88.9 us; the launch traced here: 88.7 us
  Pallas kernels  87.3 us (98%)
  between operations  1.45 us (2%)
    pallas_call x1, Pallas kernels, call_layer(): pl.pallas_call(functools.partial(layer_kernel, cells, fsdp, factor), out_...  83.5 us
    pallas_call x1, Pallas kernels, call_layer(): pl.pallas_call(finish_kernel, out_shape=[jax.ShapeDtypeStruct(s, t) for s...  3.81 us

profile of v3, /device:TPU:0, one launch (start us, length us, event | category | flops | bytes accessed | tf_op | source)
XLA Modules:
  0.0 88.7 jit_solution(2507941773651142786)
XLA Ops:
  1.3 83.5 %layer.1 = (bf16[1024,512]{1,0:T(8,128)(2,1)}, f32[1024,512]{1,0:T(8,128)}, bf16[128,3072]{1,0:T(8,128)(2,1)}, f32[16,128]{1,0:T(8,128)}) custom-call(s32[1]{0:T(128)S(6)} %copy.18.len_ref, s32[1,1024]{1,0:T(1,128)} %gen_in.1, bf16[1024,512]{1,0:T(8,128)(2,1)} %bitcast.4, bf16[1024,512]{1,0:T(8,128)(2,1)} %bitcast.5, bf16[128,1536]{1,0:T(8,128)(2,1)} %wq_in.1, ...), custom_call_target="tpu_custom_call" | custom-call | tf_op jit(solution)/shard_map/layer/pallas_call | solution.py:822
  84.7 3.8 %finish.1 = (bf16[1024,512]{1,0:T(8,128)(2,1)}, f32[1024,512]{1,0:T(8,128)}, f32[128,1536]{1,0:T(8,128)}, f32[128,512]{1,0:T(8,128)}, f32[128,512]{1,0:T(8,128)}...) custom-call(bf16[1024,512]{1,0:T(8,128)(2,1)} %get-tuple-element.20.mixed_in, ...), custom_call_target="tpu_custom_call" | custom-call | tf_op jit(solution)/shard_map/finish/pallas_call | solution.py:838

commit v4 on v3

--- a/solution.py
+++ b/solution.py
@@ -485,13 +485,17 @@
         to = lax.rem(low + k, group)
         rows = pl.ds(aligned(lax.rem(to, near) * band + lax.div(to, near) * piece, piece), piece)
         slot = k - 1 if s is shard else group - 1 + k
-        return remote(G.at[s, rows, cols], R6.at[slot], s6s.at[0], s6r.at[0], (high * group + to, s))
+        which = c[0] - 2
+        return remote(
+            G.at[s, rows, cols], R6.at[which, slot], s6s.at[which], s6r.at[which], (high * group + to, s)
+        )
 
     def d_all(c):
         return [d_one(c, k, s_far) for k in range(group)] + [d_one(c, k, shard) for k in range(1, group)]
 
     def d_whole(c):
-        return remote(R6, R6, s6s.at[0], s6r.at[0], low_dev(1))
+        which = c[0] - 2
+        return remote(R6.at[which], R6.at[which], s6s.at[which], s6r.at[which], low_dev(1))
 
     def pair_sum(c):
         i, cols = cols_of(c)
@@ -510,7 +514,7 @@
         total = G[shard, own_rows, cols].astype(F32)
         d_whole(c).wait_recv()
         for k in range(2 * group - 1):
-            total = total + R6[k].astype(F32)
+            total = total + R6[c[0] - 2, k].astype(F32)
         share(c, total)
 
     halved = [0, 1, 2, 3, (0,), (1,)]
@@ -520,17 +524,22 @@
         for c in halved + direct:
             for copy in s1_all(c):
                 copy.wait_send()
-        for c in halved + direct[:1]:
+        for c in halved:
             for copy in s2_all(c):
                 copy.wait_send()
         for c in halved:
             h3_copy(c).wait_send()
             h4_copy(c).wait_send()
             h5_whole(c).wait_send()
-        s3_whole(direct[0]).wait_send()
-        d_whole(direct[1]).wait_send()
+        for c in range(parts):
+            w_copy(c, shard, 1, fsdp_dev(s_far)).wait_send()
+            w_copy(c, shard, 0, fsdp_dev(s_near)).wait_send()
+            w_copy(c, s_far, 2, fsdp_dev(s_near)).wait_send()
+        for i, s in enumerate(others):
+            vec_copy(i, s).wait_send()
+            v1_copy(i, s).wait_send()
         for c in direct:
-            s4_whole(c).wait_send()
+            d_whole(c).wait_send()
 
     for i, (left, right) in enumerate(((att, gbr), (nl, gb), (act, gf))):
         term = (dot(left[...].T, right[...]) * factor).astype(BF)
@@ -608,15 +617,19 @@
     vecg[1:2, :] = col_sum(all_dv.astype(F32))
 
     def backward_pair(p, _):
-        before = jnp.maximum(p - 1, 0)
+        opening = isinstance(p, int) and p == 0
+        before = p - 1
         for n in range(per_head):
-            key_grads(before, 1, n, Z1)
+            if not opening:
+                key_grads(before, 1, n, Z1)
             if n == 0:
-                query_grads(before, 1, per_head - 1, Z1)
+                if not opening:
+                    query_grads(before, 1, per_head - 1, Z1)
             else:
                 query_grads(p, 0, n - 1, Z0)
             score_grads(p, 0, n, Z0)
-        pair_end(before)
+        if not opening:
+            pair_end(before)
         pl.when(p == 0)(lambda: s2_start(3))
         pl.when(p == 1)(lambda: h3_start(2))
         pl.when(p >= 2)(lambda: s2_start((p - 2,)))
@@ -632,9 +645,9 @@
             else:
                 query_grads(p, 1, n - 1, Z1)
             score_grads(p, 1, n, Z1)
-            if n == 0:
+            if n == 0 and not opening:
                 pair_term(before)
-            if n == 2:
+            if n == 1:
                 pl.when(p >= 1)(lambda: s1_start((p - 1,)))
         pl.when(p == 0)(lambda: h3_start(1))
         pl.when(p == 0)(lambda: h4_start(0))
@@ -643,9 +656,10 @@
         pl.when(p == 2)(lambda: h5_start(1))
         return 0
 
-    lax.fori_loop(0, pairs, backward_pair, 0)
+    backward_pair(0, 0)
+    lax.fori_loop(1, pairs, backward_pair, 0)
     last = pairs - 1
-    s2_start((2,))
+    d_start((2,))
     for n in range(per_head):
         key_grads(last, 1, n, Z1)
     query_grads(last, 1, per_head - 1, Z1)
@@ -690,10 +704,9 @@
     V1[...] = V0[shard] + VR1[0] + VR1[1] + VR1[2]
     for r in range(1, group):
         v2_copy(r).start()
-    s3_start((2,))
+    d4_start((2,))
     h5_start((1,))
     d4_start((3,))
-    s4_start((2,))
     total = V1[...]
     for r in range(1, group):
         v2_copy(r).wait_recv()
@@ -708,6 +721,7 @@
     VR1[0] = total
     vec_end = pltpu.make_async_copy(VR1.at[0], vec_out, out_sem.at[2])
     vec_end.start()
+    drain()
     for c in halved:
         h5_whole(c).wait_recv()
     early = 5 * width
@@ -719,15 +733,8 @@
     late_copy = pltpu.make_async_copy(R4.at[:, late_cols], sums_out.at[:, late_cols], out_sem.at[4])
     late_copy.start()
 
-    for c in range(parts):
-        w_copy(c, shard, 1, fsdp_dev(s_far)).wait_send()
-        w_copy(c, shard, 0, fsdp_dev(s_near)).wait_send()
-        w_copy(c, s_far, 2, fsdp_dev(s_near)).wait_send()
-
-    drain()
-    for i, s in enumerate(others):
-        vec_copy(i, s).wait_send()
-        v1_copy(i, s).wait_send()
+    for c in direct:
+        s4_whole(c).wait_send()
     for r in range(1, group):
         v2_copy(r).wait_send()
     for r in range(1, far):
@@ -751,34 +758,33 @@
         copy.start()
         return copy
 
+    ins.append(start(sums_in, R))
+    ins.append(start(vec_in, V))
     for i in range(steps):
         part = pl.ds(i * rows, rows)
         ins.append(start(tgrad_in.at[part], T.at[part]))
         ins.append(start(mixed_in.at[part], M.at[part]))
-    ins.append(start(sums_in, R))
-    ins.append(start(vec_in, V))
-    for i in range(steps):
-        part = pl.ds(i * rows, rows)
-        ins[2 * i].wait()
-        outs.append(start(T.at[part], tgrad_out.at[part]))
-        ins[2 * i + 1].wait()
-        outs.append(start(M.at[part], mixed_out.at[part]))
-    ins[2 * steps].wait()
+    ins[0].wait()
     for p in range(pairs):
         for t in range(2):
             c = 4 * width + 256 * p + 128 * t
             Q[:, t * width + p * 128 : t * width + p * 128 + 128] = R[:, c : c + 128].astype(F32)
     Q[:, 2 * width :] = R[:, 3 * width : 4 * width].astype(F32)
     outs.append(start(Q, qkv_out))
-    for i, ref in enumerate((O, A, B)):
+    for i, (ref, to) in enumerate(((O, wo_out), (A, w1_out), (B, w2_out))):
         ref[...] = R[:, i * width : i * width + width].astype(F32)
-    for src, dst in ((O, wo_out), (A, w1_out), (B, w2_out)):
-        outs.append(start(src, dst))
-    ins[2 * steps + 1].wait()
+        outs.append(start(ref, to))
+    ins[1].wait()
     bias[...] = V[0:7, :]
     gain[...] = V[8:10, :]
     outs.append(start(bias, bias_out))
     outs.append(start(gain, gain_out))
+    for i in range(steps):
+        part = pl.ds(i * rows, rows)
+        ins[2 + 2 * i].wait()
+        outs.append(start(T.at[part], tgrad_out.at[part]))
+        ins[3 + 2 * i].wait()
+        outs.append(start(M.at[part], mixed_out.at[part]))
     for copy in outs:
         copy.wait()
 
@@ -811,13 +817,13 @@
         ((16, width), F32),
         ((fsdp, 128, 6 * width), BF), ((2, 128, 6 * width), BF), ((2 * near - 1, band, 6 * width), BF),
         (((stride - 1) * piece, 6 * width), BF), ((far_n, 2 * piece, 2 * width), BF), ((128, 6 * width), BF),
-        ((2 * piece, 6 * width), BF), ((2 * group - 1, piece, 256), BF),
+        ((2 * piece, 6 * width), BF), ((2, 2 * group - 1, piece, 256), BF),
         ((fsdp, 16, 128), F32), ((fsdp - 1, 16, 128), F32), ((16, 128), F32), ((group - 1, 16, 128), F32),
         ((16, 128), F32), ((far_n, 16, 128), F32),
     ]
     sems = [
         (18,), (5,), (5, 3), (5, 3), (3,), (3,), (8, 2), (8, 2), (8, 2 * near - 1), (8, 2 * near - 1), (8,), (8,),
-        (8, far_n), (8, far_n), (8,), (8,), (8,), (8,), (1,), (1,), (3,), (3,), (group - 1,), (group - 1,), (far_n,), (far_n,),
+        (8, far_n), (8, far_n), (8,), (8,), (8,), (8,), (2,), (2,), (3,), (3,), (group - 1,), (group - 1,), (far_n,), (far_n,),
     ]
     results = pl.pallas_call(
         functools.partial(layer_kernel, cells, fsdp, factor),

time: 88.9 us -> 87.3 us (0.982)
  Pallas kernels: 87.3 us -> 85.6 us
    pallas_call x1, Pallas kernels: 83.5 us -> 82 us  [call_layer(): pl.pallas_call(functools.partial(layer_kernel, cells, fsdp, factor), out_...]
where the time goes in v4:
time: 87.3 us; the launch traced here: 87.1 us
  Pallas kernels  85.6 us (98%)
  between operations  1.45 us (2%)
    pallas_call x1, Pallas kernels, call_layer(): pl.pallas_call(functools.partial(layer_kernel, cells, fsdp, factor), out_...  82 us
    pallas_call x1, Pallas kernels, call_layer(): pl.pallas_call(finish_kernel, out_shape=[jax.ShapeDtypeStruct(s, t) for s...  3.6 us

profile of v4, /device:TPU:0, one launch (start us, length us, event | category | flops | bytes accessed | tf_op | source)
XLA Modules:
  0.0 87.1 jit_solution(11049076340110547144)
XLA Ops:
  1.3 82.0 %layer.1 = (bf16[1024,512]{1,0:T(8,128)(2,1)}, f32[1024,512]{1,0:T(8,128)}, bf16[128,3072]{1,0:T(8,128)(2,1)}, f32[16,128]{1,0:T(8,128)}) custom-call(s32[1]{0:T(128)S(6)} %copy.18.len_ref, s32[1,1024]{1,0:T(1,128)} %gen_in.1, bf16[1024,512]{1,0:T(8,128)(2,1)} %bitcast.4, bf16[1024,512]{1,0:T(8,128)(2,1)} %bitcast.5, bf16[128,1536]{1,0:T(8,128)(2,1)} %wq_in.1, ...), custom_call_target="tpu_custom_call" | custom-call | tf_op jit(solution)/shard_map/layer/pallas_call | solution.py:828
  83.3 3.6 %finish.1 = (bf16[1024,512]{1,0:T(8,128)(2,1)}, f32[1024,512]{1,0:T(8,128)}, f32[128,1536]{1,0:T(8,128)}, f32[128,512]{1,0:T(8,128)}, f32[128,512]{1,0:T(8,128)}...) custom-call(bf16[1024,512]{1,0:T(8,128)(2,1)} %get-tuple-element.20.mixed_in, ...), custom_call_target="tpu_custom_call" | custom-call | tf_op jit(solution)/shard_map/finish/pallas_call | solution.py:844

commit v5 on v4

--- a/solution.py
+++ b/solution.py
@@ -580,11 +580,12 @@
 
     def value_grads(p, _):
         cols = pl.ds(aligned(p * CHUNK + 256, 128), 128)
-        for n in range(per_head):
-            rows = pl.ds(n * LB, LB)
+        wide = lax.broadcasted_iota(jnp.int32, (2 * LB, 128), 1) < 64
+        for n in range(per_head // 2):
+            rows = pl.ds(n * 2 * LB, 2 * LB)
             dv0 = dot(e[2 * p, rows, :], dAn[p])
             dv1 = dot(e[2 * p + 1, rows, :], dAn[p])
-            A5[rows, cols] = jnp.where(first, dv0, dv1).astype(BF)
+            A5[rows, cols] = jnp.where(wide, dv0, dv1).astype(BF)
         return 0
 
     def key_grads(p, hh, n, z_ref):

time: 87.3 us -> 87.2 us (level)
  no operation moved by 1% of the time
where the time goes in v5:
time: 87.2 us; the launch traced here: 87 us
  Pallas kernels  85.5 us (98%)
  between operations  1.45 us (2%)
    pallas_call x1, Pallas kernels, call_layer(): pl.pallas_call(functools.partial(layer_kernel, cells, fsdp, factor), out_...  81.9 us
    pallas_call x1, Pallas kernels, call_layer(): pl.pallas_call(finish_kernel, out_shape=[jax.ShapeDtypeStruct(s, t) for s...  3.6 us

profile of v5, /device:TPU:0, one launch (start us, length us, event | category | flops | bytes accessed | tf_op | source)
XLA Modules:
  0.0 87.0 jit_solution(14348773367092479341)
XLA Ops:
  1.3 81.9 %layer.1 = (bf16[1024,512]{1,0:T(8,128)(2,1)}, f32[1024,512]{1,0:T(8,128)}, bf16[128,3072]{1,0:T(8,128)(2,1)}, f32[16,128]{1,0:T(8,128)}) custom-call(s32[1]{0:T(128)S(6)} %copy.18.len_ref, s32[1,1024]{1,0:T(1,128)} %gen_in.1, bf16[1024,512]{1,0:T(8,128)(2,1)} %bitcast.4, bf16[1024,512]{1,0:T(8,128)(2,1)} %bitcast.5, bf16[128,1536]{1,0:T(8,128)(2,1)} %wq_in.1, ...), custom_call_target="tpu_custom_call" | custom-call | tf_op jit(solution)/shard_map/layer/pallas_call | solution.py:829
  83.2 3.6 %finish.1 = (bf16[1024,512]{1,0:T(8,128)(2,1)}, f32[1024,512]{1,0:T(8,128)}, f32[128,1536]{1,0:T(8,128)}, f32[128,512]{1,0:T(8,128)}, f32[128,512]{1,0:T(8,128)}...) custom-call(bf16[1024,512]{1,0:T(8,128)(2,1)} %get-tuple-element.20.mixed_in, ...), custom_call_target="tpu_custom_call" | custom-call | tf_op jit(solution)/shard_map/finish/pallas_call | solution.py:845
